TPU v7x, 32 devices: a whole 2x2x4 slice. The times are simulated.
32 devices in a mesh: seq: 4 (over x, core), batch: 8 (over z, y).
Axes of the slice: x: 2, y: 2, z: 4, core: 2. Of those that a mesh axis runs over, the one named last changes fastest.
Arguments:
- residual: float32 [8, 2048, 767], P('batch', 'seq'), may hold values from -6 to 6
- documents: int32 [8, 2048], P('batch', 'seq'), may hold values from 1 to 16383, as said below
- gain_one: float32 [768], replicated, may hold values from 0.25 to 1.75
- gain_two: float32 [768], replicated, may hold values from 0.25 to 1.75
- w_qkv: bfloat16 [768, 2304], replicated, may hold values from -0.3125 to 0.3125
- w_out: bfloat16 [768, 768], replicated, may hold values from -0.4375 to 0.4375
- w_up: bfloat16 [768, 3072], replicated, may hold values from -0.21875 to 0.21875
- w_down: bfloat16 [3072, 768], replicated, may hold values from -0.109375 to 0.109375
- cotangent: float32 [8, 2048, 767], P('batch', 'seq'), may hold values from -6 to 6
Outputs:
- new_residual: float32 [8, 2048, 767], P('batch', 'seq')
- residual_grad: float32 [8, 2048, 767], P('batch', 'seq')
- gain_one_grad: float32 [768], P('seq')
- gain_two_grad: float32 [768], P('seq')
- w_qkv_grad: float32 [768, 2304], P('seq')
- w_out_grad: float32 [768, 768], P('seq')
- w_up_grad: float32 [768, 3072], P('seq')
- w_down_grad: float32 [3072, 768], P('seq')
Inputs may be any that keep to these rules, and one draw needn't show every extreme that they name: `documents`: every document is one unbroken run within a row, or the end of one row's last document followed by the start of the next row's first; the last row's last document, with id 8 * 2048 - 1, continues at the start of the first row. Within a row, ids after its first document rise. A continued document lies within the last 512 positions of the earlier row and the first 512 positions of the later one. No other document has tokens in two rows. In every row some document begins within its first 512 positions and ends within its last 512.
All inputs are finite; a program needn't handle non-finite values.
Results may differ from a plain program's by a relative error of at most 0.04.
Values may be sent and summed in bfloat16 or wider, within the bound.
A program may use at most 192 MiB of HBM per device.

v0:
```python
import functools
import math

import jax
import jax.numpy as jnp
from jax import lax
from jax.experimental import pallas as pl
from jax.experimental.pallas import tpu as pltpu
from jax.sharding import PartitionSpec as P

H = 12
HD = 64
EPSILON = 1e-06
NEG = -1e30
F32, BF16 = jnp.float32, jnp.bfloat16
VMEM_LIMIT = 60 * 2**20


def dot(a, b):
    return lax.dot_general(a, b, (((1,), (0,)), ((), ())), preferred_element_type=F32)


def dot_nt(a, b):
    return lax.dot_general(a, b, (((1,), (1,)), ((), ())), preferred_element_type=F32)


def dot_tn(a, b):
    return lax.dot_general(a, b, (((0,), (0,)), ((), ())), preferred_element_type=F32)


def expand(narrow):
    return jnp.concatenate([narrow, -jnp.sum(narrow, axis=0, keepdims=True)], axis=0)


def shrink(full_vec):
    return full_vec[:-1] - jnp.mean(full_vec, axis=0, keepdims=True)


def shrink_back(grad_narrow):
    padded = jnp.concatenate([grad_narrow, jnp.zeros_like(grad_narrow[:1])], axis=0)
    return padded - jnp.sum(grad_narrow, axis=0, keepdims=True) / padded.shape[0]


def root(full_vec):
    return lax.rsqrt(jnp.mean(full_vec * full_vec, axis=0, keepdims=True) + EPSILON)


def norm_back(narrow, gain, grad_h):
    full_vec = expand(narrow)
    r = root(full_vec)
    scaled = gain * grad_h
    grad_full = r * (scaled - full_vec * (r * r * jnp.mean(scaled * full_vec, axis=0, keepdims=True)))
    return grad_full[:-1] - grad_full[-1:]


def column(gain_ref):
    return jnp.broadcast_to(gain_ref[...], (8, gain_ref.shape[1])).T[:, 0:1]


MESH = pl.DeviceIdType.MESH


class Place:
    def __init__(self, n):
        self.s = lax.axis_index("seq")
        self.b = lax.axis_index("batch")
        self.core = lax.rem(self.s, 2)
        self.chip = self.s // 2
        self.y = lax.rem(self.b, 2)
        self.z = lax.rem(self.b // 2, 4)
        self.far = self.b // 8
        self.n = n

    def core_mate(self):
        return (self.s + 1 - 2 * self.core, self.b)

    def chip_mate(self):
        return (self.s + 2 - 4 * self.chip, self.b)

    def cross_mate(self):
        return (3 - self.s, self.b)

    def y_mate(self):
        return (self.s, self.b + 1 - 2 * self.y)

    def z_of(self, d):
        return lax.rem(self.z + d, 4)

    def z_mate(self, d):
        return (self.s, self.b + 2 * (self.z_of(d) - self.z))

    def far_mate(self, d):
        f = lax.rem(self.far + d, self.n // 8)
        return (self.s, self.b + 8 * (f - self.far))

    def next_row(self):
        return (self.s, lax.rem(self.b + 1, self.n))

    def prior_row(self):
        return (self.s, lax.rem(self.b + self.n - 1, self.n))

    def all_mates(self):
        mates = [self.core_mate(), self.chip_mate(), self.cross_mate(), self.y_mate()]
        mates += [self.z_mate(d) for d in (1, 2, 3)]
        mates += [self.far_mate(d) for d in range(1, self.n // 8)]
        return mates + [self.next_row(), self.prior_row()]


def greet(mates):
    barrier = pltpu.get_barrier_semaphore()
    for mate in mates:
        pl.semaphore_signal(barrier, inc=1, device_id=mate, device_id_type=MESH)
    pl.semaphore_wait(barrier, len(mates))


class Copies:
    def __init__(self, sems):
        self.sems, self.made = sems, {}

    def remote(self, name, src, dst, mate):
        k = len(self.made)

        def make():
            return pltpu.make_async_remote_copy(
                src_ref=src(),
                dst_ref=dst(),
                send_sem=self.sems.at[0, k],
                recv_sem=self.sems.at[1, k],
                device_id=mate(),
                device_id_type=MESH,
            )

        self.made[name] = make

    def local(self, name, src, dst):
        k = len(self.made)

        def make():
            return pltpu.make_async_copy(src(), dst(), self.sems.at[0, k])

        self.made[name] = make

    def start(self, *names):
        for name in names:
            self.made[name]().start()

    def wait(self, *names):
        for name in names:
            self.made[name]().wait()

    def wait_recv(self, *names):
        for name in names:
            self.made[name]().wait_recv()

    def wait_send(self, *names):
        for name in names:
            self.made[name]().wait_send()


def rows_at(at, count):
    return pl.ds(pl.multiple_of(at, 16), count)


def blockwise(rows, body):
    step = next(s for s in (48, 32, 16) if rows % s == 0)

    def one(i, carry):
        body(i * step, step)
        return carry

    lax.fori_loop(0, rows // step, one, 0)


class Sum:
    def __init__(self, place, copies, name, mode, src, first, rows, cols, bufs, out):
        self.p, self.c, self.name, self.mode = place, copies, name, mode
        self.src, self.first, self.rows, self.cols, self.out = src, first, rows, cols, out
        self.own, self.ry, self.rz, self.res, self.rf = bufs[:5]
        self.rc = bufs[5] if mode == "whole" else None
        self.rx = bufs[-1] if mode != "share" else None
        self.mine = (lambda: self.own.at[self.p.chip]) if mode == "whole" else (lambda: self.own.at[0])
        self.define()

    def define(self):
        p, c, half, quarter, far = self.p, self.c, self.rows // 2, self.rows // 8, self.p.n // 8
        if self.mode == "whole":
            first = pl.ds(self.first, self.rows)
            for order in (1, 0):
                chip = lambda order=order: lax.rem(p.chip + order, 2)
                c.remote(
                    self.id(("core", order)),
                    lambda chip=chip: self.src.at[2 * chip() + 1 - p.core, first],
                    lambda chip=chip: self.rc.at[chip()],
                    p.core_mate,
                )
                c.local(
                    self.id(("own", order)),
                    lambda chip=chip: self.src.at[2 * chip() + p.core, first],
                    lambda chip=chip: self.own.at[chip()],
                )
            c.remote(self.id("x"), lambda: self.own.at[1 - p.chip], lambda: self.rx, p.chip_mate)
        elif self.mode == "pair":
            c.remote(self.id("x"), lambda: self.src.at[1 - p.chip], lambda: self.rx, p.chip_mate)
            c.local(self.id("own"), lambda: self.src.at[p.chip], lambda: self.own.at[0])
        elif self.src is not None:
            c.local(self.id("own"), lambda: self.src, lambda: self.own.at[0])
        other_half = lambda: self.mine().at[rows_at((1 - p.y) * half, half)]
        c.remote(self.id("y"), other_half, lambda: self.ry, p.y_mate)
        for d in (2, 1, 3):
            c.remote(
                self.id(("z", d)),
                lambda d=d: self.mine().at[rows_at(p.y * half + p.z_of(d) * quarter, quarter)],
                lambda d=d: self.rz.at[3 - d],
                lambda d=d: p.z_mate(d),
            )
        spot = lambda: self.res.at[rows_at(p.y * half + p.z * quarter, quarter)]
        for d in range(1, far):
            c.remote(
                self.id(("far", d)), spot, lambda d=d: self.rf.at[far - d - 1], lambda d=d: p.far_mate(d)
            )
        for d in (2, 1, 3):
            c.remote(self.id(("back z", d)), spot, spot, lambda d=d: p.z_mate(d))
        my_half = lambda: self.res.at[rows_at(p.y * half, half)]
        c.remote(self.id("back y"), my_half, my_half, p.y_mate)
        for k, (src, dst) in enumerate(self.out):
            c.local(self.id(("out", k)), lambda src=src: self.res.at[src], lambda dst=dst: dst)

    @staticmethod
    def scratch(mode, rows, cols, n):
        def v(*s):
            return pltpu.VMEM(s, BF16)

        whole = mode == "whole"
        out = [v(2 if whole else 1, rows, cols), v(rows // 2, cols), v(3, rows // 8, cols), v(rows, cols)]
        out.append(v(max(n // 8 - 1, 1), rows // 8, cols))
        out += [v(2, rows, cols)] if whole else []
        return out + ([v(rows, cols)] if mode != "share" else [])

    def id(self, what):
        return (self.name, what)

    def p0(self):
        if self.mode == "pair":
            self.c.start(self.id("x"), self.id("own"))
        elif self.mode == "share" and self.src is not None:
            self.c.start(self.id("own"))
        if self.mode != "whole":
            return
        for order in (1, 0):
            self.c.start(self.id(("core", order)), self.id(("own", order)))

    def add_core(self, chip):
        def body(at, step):
            rows = rows_at(at, step)
            total = self.own[chip, rows, :].astype(F32) + self.rc[chip, rows, :].astype(F32)
            self.own[chip, rows, :] = total.astype(BF16)

        blockwise(self.rows, body)

    def p1(self):
        p = self.p
        self.c.wait(self.id(("core", 1)), self.id(("own", 1)))
        self.add_core(1 - p.chip)
        self.c.start(self.id("x"))
        self.c.wait(self.id(("core", 0)), self.id(("own", 0)))
        self.add_core(p.chip)

    def add_x(self, first):
        own = self.mine()

        def body(at, step):
            rows = rows_at(first + at, step)
            own[rows, :] = (own[rows, :].astype(F32) + self.rx[rows, :].astype(F32)).astype(BF16)

        blockwise(self.rows // 2, body)

    def p2(self):
        p, half = self.p, self.rows // 2
        if self.mode == "pair" or self.mode == "share" and self.src is not None:
            self.c.wait(self.id("own"))
        if self.mode != "share":
            self.c.wait(self.id("x"))
            self.add_x((1 - p.y) * half)
        self.c.start(self.id("y"))
        if self.mode != "share":
            self.add_x(p.y * half)

    def p3(self):
        p, half = self.p, self.rows // 2
        self.c.wait(self.id("y"))
        own = self.mine()

        def body(at, step):
            rows = rows_at(p.y * half + at, step)
            total = own[rows, :].astype(F32) + self.ry[rows_at(at, step), :].astype(F32)
            own[rows, :] = total.astype(BF16)

        blockwise(half, body)
        self.c.start(*[self.id(("z", d)) for d in (2, 1, 3)])

    def p4(self):
        p, half, quarter = self.p, self.rows // 2, self.rows // 8
        self.c.wait(*[self.id(("z", d)) for d in (1, 2, 3)])
        own = self.mine()
        base = p.y * half + p.z * quarter

        def body(at, step):
            rows = rows_at(base + at, step)
            total = own[rows, :].astype(F32)
            for d in range(3):
                total = total + self.rz[d, rows_at(at, step), :].astype(F32)
            self.res[rows, :] = total.astype(BF16)

        blockwise(quarter, body)
        far = p.n // 8
        if far > 1:
            self.c.start(*[self.id(("far", d)) for d in range(1, far)])
            self.c.wait(*[self.id(("far", d)) for d in range(1, far)])

            def more(at, step):
                rows = rows_at(base + at, step)
                total = self.res[rows, :].astype(F32)
                for d in range(far - 1):
                    total = total + self.rf[d, rows_at(at, step), :].astype(F32)
                self.res[rows, :] = total.astype(BF16)

            blockwise(quarter, more)
        self.c.start(*[self.id(("back z", d)) for d in (2, 1, 3)])

    def p5(self):
        self.c.wait(*[self.id(("back z", d)) for d in (1, 2, 3)])
        self.c.start(self.id("back y"))

    def p6(self):
        self.c.wait(self.id("back y"))
        self.c.start(*[self.id(("out", k)) for k in range(len(self.out))])

    def p7(self):
        self.c.wait(*[self.id(("out", k)) for k in range(len(self.out))])


def fore_kernel(n, tok, blocks, heads, *refs):
    x, gain, docs, w = refs[:4]
    attT_o, hT_o, kT_o, qT_o, oT_o, lse_o, start_o, k_o, v_o, wm_o = refs[4:14]
    xs, ws, wm, hT, docs_all, prior_docs, start, kT, vT, qT, kk, vv, acc, m_ref, l_ref, lse, stage, sems = refs[14:]
    width = xs.shape[0] + 1
    row = blocks * tok
    mine = heads * HD
    p = Place(n)
    c = Copies(sems)
    mates = {"core": p.core_mate, "chip": p.chip_mate, "cross": p.cross_mate}
    block = lambda at: pl.ds(pl.multiple_of(at * tok, tok), tok)
    here = lambda: block(p.s)
    c.local("x", lambda: x.at[:, 0, :], lambda: xs)
    c.local("w", lambda: w, lambda: ws)
    c.local("docs", lambda: docs, lambda: docs_all.at[:, here()])
    for name, mate in mates.items():
        c.remote(("docs", name), lambda: docs, lambda: docs_all.at[:, here()], mate)
    last = pl.ds(row - tok, tok)
    c.remote("prior docs", lambda: docs_all.at[:, last], lambda: prior_docs, p.next_row)
    c.remote("h core", lambda: hT.at[:, here()], lambda: hT.at[:, here()], p.core_mate)
    half = tok // 2
    for k in range(2):
        piece = lambda s, k=k: hT.at[:, pl.ds(pl.multiple_of(s * tok + k * half, half), half)]
        c.remote(("h chip", k), lambda piece=piece: piece(p.s), lambda piece=piece: piece(p.s), p.chip_mate)
        other = lambda piece=piece: piece(p.chip_mate()[0])
        c.remote(("h on", k), other, other, p.core_mate)
    end = pl.ds(row, tok)
    c.remote("prior k", lambda: kT.at[:, end], lambda: kT.at[:, 0:tok], p.next_row)
    c.remote("prior v", lambda: vT.at[:, end], lambda: vT.at[:, 0:tok], p.next_row)
    for h in range(heads):
        spot = lambda h=h: attT_o.at[pl.ds(pl.multiple_of(p.s * mine + h * HD, HD), HD)]
        for name, mate in mates.items():
            src = lambda h=h, mate=mate: stage.at[pl.ds(h * HD, HD), block(mate()[0])]
            c.remote(("att", h, name), src, spot, mate)
        c.local(("att", h, "own"), lambda h=h: stage.at[pl.ds(h * HD, HD), here()], spot)
    outs = {"hT": (hT, hT_o), "kT": (kT, kT_o), "qT": (qT, qT_o), "oT": (acc, oT_o), "lse": (lse, lse_o)}
    outs.update({"start": (start, start_o), "k": (kk, k_o), "v": (vv, v_o), "wm": (wm, wm_o)})
    for name, (src, dst) in outs.items():
        c.local(("out", name), lambda src=src: src, lambda dst=dst: dst)

    c.start("x", "docs", "w")
    greet([p.core_mate(), p.chip_mate(), p.cross_mate(), p.next_row(), p.prior_row()])
    c.start(*[("docs", name) for name in mates])
    c.wait("x")
    full_vec = expand(xs[...])
    hT[:, here()] = (column(gain) * full_vec * root(full_vec)).astype(BF16)
    c.start(("h chip", 0), "h core")
    c.start(("h chip", 1))

    c.wait("w")
    for s in range(blocks):
        @pl.when(p.s == s)
        def _():
            for h in range(heads):
                for k in range(3):
                    at = k * width + s * mine + h * HD
                    to = (h * 3 + k) * HD
                    wm[:, to : to + HD] = ws[:, at : at + HD]

    c.wait("docs", *[("docs", name) for name in mates])
    c.start("prior docs")
    ids = jnp.broadcast_to(docs_all[...], (8, row))
    pos = lax.broadcasted_iota(jnp.int32, (8, row), 1)
    since = jnp.where((ids != pltpu.roll(ids, 1, 1)) | (pos == 0), pos, 0)
    hop = 1
    while hop < row:
        since = jnp.maximum(since, jnp.where(pos >= hop, pltpu.roll(since, hop, 1), 0))
        hop *= 2
    start[...] = since[0:1] + tok
    m_ref[...] = jnp.full(m_ref.shape, NEG, F32)
    l_ref[...] = jnp.zeros(l_ref.shape, F32)
    acc[...] = jnp.zeros(acc.shape, F32)

    def natural(keys_at):
        keys = pl.ds(pl.multiple_of(keys_at, tok), tok)
        for h in range(heads):
            kk[h, keys, :] = kT[h * HD : (h + 1) * HD, keys].T
            vv[h, keys, :] = vT[h * HD : (h + 1) * HD, keys].T

    def project(at):
        packed = dot_tn(wm[...], hT[:, block(at)]).astype(BF16)
        keys = pl.ds(pl.multiple_of((at + 1) * tok, tok), tok)
        for h in range(heads):
            to, base = slice(h * HD, (h + 1) * HD), h * 3 * HD
            qT[to, block(at)] = packed[base : base + HD] * jnp.bfloat16(1.0 / math.sqrt(HD))
            kT[to, keys] = packed[base + HD : base + 2 * HD]
            vT[to, keys] = packed[base + 2 * HD : base + 3 * HD]
        natural((at + 1) * tok)

    def pair(h, q0, qw, k0, kw, causal):
        hr = pl.ds(pl.multiple_of(h * HD, HD), HD)
        qs, ks = pl.ds(pl.multiple_of(q0, 128), qw), pl.ds(pl.multiple_of(k0, 128), kw)
        s = dot(kk[h, ks, :], qT[hr, qs])
        at = lax.broadcasted_iota(jnp.int32, s.shape, 0) + k0
        keep = at >= start[:, qs]
        if causal:
            until = lax.broadcasted_iota(jnp.int32, s.shape, 1) + (q0 + tok)
            keep = keep & (at <= until)
        s = jnp.where(keep, s, NEG)
        m = m_ref[h, :, qs]
        new_m = jnp.maximum(m, jnp.max(s, axis=0, keepdims=True))
        e = jnp.exp(s - new_m)
        shift = jnp.exp(m - new_m)
        m_ref[h, :, qs] = new_m
        l_ref[h, :, qs] = l_ref[h, :, qs] * shift + jnp.sum(e, axis=0, keepdims=True)
        acc[hr, qs] = acc[hr, qs] * shift + dot(vT[hr, ks], e.astype(BF16))

    def within(h, first):
        def one(t, carry):
            at = (first + t) * tok
            pair(h, at, tok, at + tok, half, True)
            pair(h, at + half, half, at + tok + half, half, True)
            return carry

        lax.fori_loop(0, 2, one, 0)

    def finish(h, i):
        hr, qs = pl.ds(pl.multiple_of(h * HD, HD), HD), block(i)
        out = acc[hr, qs] / l_ref[h, :, qs]
        acc[hr, qs] = out
        stage[hr, qs] = out.astype(BF16)
        lse[h, :, qs] = m_ref[h, :, qs] + jnp.log(l_ref[h, :, qs])

    def send_att(h, zero):
        for name, mate in list(mates.items()) + [("own", lambda: (p.s,))]:
            @pl.when((mate()[0] == 0) == zero)
            def _():
                c.start(("att", h, name))

    near, far = 2 * p.chip, 2 * (1 - p.chip)
    c.wait_recv("h core")

    def project_near(t, carry):
        project(near + t)
        return carry

    lax.fori_loop(0, 2, project_near, 0)

    @pl.when(p.chip == 1)
    def _():
        c.start("prior k", "prior v")

    def first(h, carry):
        within(h, near)
        pair(h, (near + 1) * tok, tok, (near + 1) * tok, tok, False)
        return carry

    lax.fori_loop(0, heads, first, 0)
    for k in range(2):
        c.wait_recv(("h chip", k))
        c.start(("h on", k))
    project(p.chip_mate()[0])
    c.wait_recv(("h on", 0), ("h on", 1))
    project(p.cross_mate()[0])

    @pl.when(p.chip == 0)
    def _():
        c.start("prior k", "prior v")

    def second(h, carry):
        within(h, far)
        pair(h, (far + 1) * tok, tok, (far + 1) * tok, tok, False)

        def cross(t, carry):
            pair(h, (2 + t // 2) * tok, tok, (1 + t % 2) * tok, tok, False)
            return carry

        lax.fori_loop(0, 4, cross, 0)
        lax.fori_loop(1, blocks, lambda i, carry: (finish(h, i), carry)[1], 0)
        for k in range(heads):
            @pl.when(h == k)
            def _():
                send_att(k, False)
        return carry

    lax.fori_loop(0, heads, second, 0)
    c.wait_recv("prior docs")
    from_doc = docs_all[:, 0:1]
    at = lax.broadcasted_iota(jnp.int32, (1, tok), 1)
    run = jnp.max(jnp.where(prior_docs[...] != from_doc, at + 1, 0), axis=1, keepdims=True)
    start[:, 0:tok] = jnp.where(start[:, 0:tok] == tok, run, start[:, 0:tok])
    c.wait_recv("prior k", "prior v")
    natural(0)

    def third(h, carry):
        pair(h, 0, tok, 0, tok, False)
        finish(h, 0)
        for k in range(heads):
            @pl.when(h == k)
            def _():
                send_att(k, True)
        return carry

    lax.fori_loop(0, heads, third, 0)
    c.start(*[("out", name) for name in outs])
    c.wait_send("h core", ("h chip", 0), ("h chip", 1), ("h on", 0), ("h on", 1), "prior docs", "prior k", "prior v")
    for h in range(heads):
        c.wait(*[("att", h, name) for name in list(mates) + ["own"]])
    c.wait(*[("out", name) for name in outs])


def fore_pass(n, tok, blocks, x, gain, docs, w):
    width, heads = w.shape[0], H // blocks
    row, mine = blocks * tok, heads * HD
    v = lambda *s, t=BF16: pltpu.VMEM(s, t)
    o = lambda *s, t=BF16: jax.ShapeDtypeStruct(s, t)
    hbm = pl.BlockSpec(memory_space=pl.ANY)
    scratch = [
        v(width - 1, tok, t=F32), v(width, 3 * width), v(width, 3 * mine), v(width, row),
        v(1, row, t=jnp.int32), v(1, tok, t=jnp.int32), v(1, row, t=jnp.int32),
        v(mine, row + tok), v(mine, row + tok), v(mine, row), v(heads, row + tok, HD), v(heads, row + tok, HD),
        v(mine, row, t=F32), v(heads, 1, row, t=F32), v(heads, 1, row, t=F32), v(heads, 1, row, t=F32), v(mine, row),
        pltpu.SemaphoreType.DMA((2, 24 + 4 * heads)),
    ]
    return pl.pallas_call(
        functools.partial(fore_kernel, n, tok, blocks, heads),
        out_shape=[
            o(width, tok), o(width, row), o(mine, row + tok), o(mine, row), o(mine, row, t=F32), o(heads, 1, row, t=F32),
            o(1, row, t=jnp.int32), o(heads, row + tok, HD), o(heads, row + tok, HD), o(width, 3 * mine),
        ],
        in_specs=[hbm, pl.BlockSpec(memory_space=pltpu.VMEM), hbm, hbm],
        out_specs=[hbm] * 10,
        scratch_shapes=scratch,
        compiler_params=pltpu.CompilerParams(collective_id=0, has_side_effects=True, vmem_limit_bytes=VMEM_LIMIT),
    )(x, gain, docs, w)


def gelu_both(v, grad):
    rate = math.sqrt(2.0 / math.pi)
    square = v * v
    th = jnp.tanh(rate * v * (1.0 + 0.044715 * square))
    up = 0.5 * (1.0 + th)
    slope = up + 0.5 * v * (1.0 - th * th) * (rate * (1.0 + 3.0 * 0.044715 * square))
    return (v * up).astype(BF16), (grad * slope).astype(BF16)


def mid_kernel(n, blocks, *refs):
    x, cot, attT, gain, w_out, w_up, w_down = refs[:7]
    new_o, gm_o, doT_o, gu_o, go_o, share_o, pair_o = refs[7:14]
    xs, cs, at, wo, wu, wd, mid, h2, g2, g1, geluT, gupT, b2, gh, dw, rc, rx, ga, gu, go, sems = refs[14:]
    tok, width = xs.shape[1], xs.shape[0] + 1
    parts = wu.shape[1] // width
    share = width // blocks
    p = Place(n)
    c = Copies(sems)
    mates = {"cross": p.cross_mate, "chip": p.chip_mate, "core": p.core_mate}
    c.local("att", lambda: attT, lambda: at)
    c.local("wo", lambda: w_out, lambda: wo)
    c.local("x", lambda: x.at[:, 0, :], lambda: xs)
    c.local("cot", lambda: cot.at[:, 0, :], lambda: cs)
    c.local("wu", lambda: w_up, lambda: wu)
    c.local("wd", lambda: w_down, lambda: wd)
    c.remote("core 0", lambda: dw.at[0], lambda: rc.at[0], p.core_mate)
    c.remote("core 1", lambda: dw.at[2], lambda: rc.at[1], p.core_mate)
    part = width // 2
    c.remote("chip", lambda: dw.at[1, 0:part], lambda: rx, p.chip_mate)
    there = lambda: doT_o.at[:, pl.ds(pl.multiple_of(p.s * tok, tok), tok)]
    for name, mate in mates.items():
        c.remote(("ga", name), lambda mate=mate: ga.at[rows_at(mate()[0] * share, share)], there, mate)
    c.local(("ga", "own"), lambda: ga.at[rows_at(p.s * share, share)], there)
    c.local("new out", lambda: xs, lambda: new_o.at[:, 0, :])
    c.local("gm", lambda: cs, lambda: gm_o)
    for k in range(parts):
        c.local(("gu", k), lambda k=k: gu.at[:, pl.ds(k * share, share)], lambda k=k: gu_o.at[:, pl.ds(k * share, share)])
    c.local("go", lambda: go, lambda: go_o)
    c.local("share", lambda: dw.at[3, 0:part], lambda: share_o)
    c.local("pair 0", lambda: dw.at[1, part:width], lambda: pair_o.at[1 - p.chip])
    c.local("pair 1", lambda: dw.at[3, part:width], lambda: pair_o.at[p.chip])

    c.start("att", "wo", "x", "cot", "wu", "wd")
    greet([p.core_mate(), p.chip_mate(), p.cross_mate()])
    c.wait("att", "wo")
    branch_one = dot_tn(wo[...], at[...])
    c.wait("x")
    mid[...] = xs[...] + shrink(branch_one)
    full_vec = expand(mid[...])
    gain_col = column(gain)
    h2[...] = (gain_col * full_vec * root(full_vec)).astype(BF16)
    c.wait("cot")
    g2[...] = shrink_back(cs[...]).astype(BF16)
    b2[...] = jnp.zeros_like(b2)
    gh[...] = jnp.zeros_like(gh)
    c.wait("wu", "wd")

    def add(dst, src, rows):
        def body(first, step):
            r = rows_at(first, step)
            dw[dst, r, :] = (dw[dst, r, :].astype(F32) + src[r, :].astype(F32)).astype(BF16)

        blockwise(rows, body)

    def piece(t, carry):
        s = jnp.where(t == 0, p.cross_mate()[0], jnp.where(t == 1, p.chip_mate()[0], jnp.where(t == 2, p.core_mate()[0], p.s)))
        its = pl.ds(pl.multiple_of(s * width, width), width)
        up = dot_tn(wu[:, its], h2[...])
        grad_gelu = dot(wd[its, :], g2[...])
        gelu, grad_up = gelu_both(up, grad_gelu)
        geluT[...] = gelu
        gupT[its, :] = grad_up
        dw[t] = dot_nt(geluT[...], g2[...]).astype(BF16)

        @pl.when(t == 0)
        def _():
            c.start("core 0")

        @pl.when(t == 2)
        def _():
            c.start("core 1")

        b2[...] += dot_tn(wd[its, :], geluT[...])
        gh[...] += dot(wu[:, its], gupT[its, :])

        @pl.when(t == 1)
        def _():
            c.wait_recv("core 0")
            add(1, rc.at[0], width)
            c.start("chip")

        return carry

    lax.fori_loop(0, parts, piece, 0)
    grad_middle = cs[...] + norm_back(mid[...], gain_col, gh[...])
    cs[...] = grad_middle
    g1[...] = shrink_back(grad_middle).astype(BF16)
    ga[...] = dot(wo[...], g1[...]).astype(BF16)
    c.start(*[("ga", name) for name in list(mates) + ["own"]])
    c.start("gm")
    xs[...] = mid[...] + shrink(b2[...])
    c.start("new out")

    def up_grad(k, carry):
        its = pl.ds(pl.multiple_of(k * width, width), width)
        grad = dot_nt(h2[...], gupT[its, :]).astype(BF16)
        for s in range(blocks):
            gu[s, rows_at(k * share, share), :] = grad[s * share : (s + 1) * share]
        return carry

    lax.fori_loop(0, parts, up_grad, 0)
    c.start(*[("gu", k) for k in range(parts)])
    out_grad = dot_nt(at[...], g1[...]).astype(BF16)
    for s in range(blocks):
        for k in range(2):
            go[s, k * share : (k + 1) * share, :] = out_grad[s * share : (s + 1) * share, k * part : (k + 1) * part]
    c.start("go")
    c.wait_recv("core 1")
    add(3, rc.at[1], width)
    c.start("pair 0", "pair 1")
    c.wait("chip")
    add(3, rx, part)
    c.start("share")
    c.wait_send("core 0", "core 1")
    c.wait(*[("ga", name) for name in list(mates) + ["own"]])
    c.wait("gm", "new out", "go", "share", "pair 0", "pair 1", *[("gu", k) for k in range(parts)])


def mid_pass(n, blocks, x, cot, attT, gain, w_out, w_up, w_down):
    width, tok = attT.shape
    parts, share = w_up.shape[1] // width, width // blocks
    v = lambda *s, t=BF16: pltpu.VMEM(s, t)
    o = lambda *s, t=BF16: jax.ShapeDtypeStruct(s, t)
    hbm = pl.BlockSpec(memory_space=pl.ANY)
    scratch = [
        v(width - 1, tok, t=F32), v(width - 1, tok, t=F32), v(width, tok), v(width, width), v(*w_up.shape), v(*w_down.shape),
        v(width - 1, tok, t=F32), v(width, tok), v(width, tok), v(width, tok), v(width, tok), v(w_up.shape[1], tok),
        v(width, tok, t=F32), v(width, tok, t=F32), v(4, width, width), v(2, width, width), v(width // 2, width),
        v(width, tok), v(blocks, parts * share, width), v(blocks, 2 * share, width // 2),
        pltpu.SemaphoreType.DMA((2, 32)),
    ]
    return pl.pallas_call(
        functools.partial(mid_kernel, n, blocks),
        out_shape=[
            o(width - 1, 1, tok, t=F32), o(width - 1, tok, t=F32), o(share, blocks * tok), o(blocks, parts * share, width),
            o(blocks, 2 * share, width // 2), o(width // 2, width), o(2, width // 2, width),
        ],
        in_specs=[hbm, hbm, hbm, pl.BlockSpec(memory_space=pltpu.VMEM), hbm, hbm, hbm],
        out_specs=[hbm] * 7,
        scratch_shapes=scratch,
        compiler_params=pltpu.CompilerParams(collective_id=2, has_side_effects=True, vmem_limit_bytes=VMEM_LIMIT),
    )(x, cot, attT, gain, w_out, w_up, w_down)


BACK_IN = ("doT", "k", "v", "kT", "qT", "oT", "lse", "start", "hT", "wm", "x", "gm")
DW = ("cross", "chip", "core", "own")


def back_kernel(n, tok, blocks, heads, parts, *refs):
    refs = list(refs)
    take = lambda count: [refs.pop(0) for _ in range(count)]
    hbm = dict(zip(BACK_IN, take(len(BACK_IN))))
    share_d, pair_d, gu, go, w_qkv, w_up, gain = take(7)
    down_o, up_o, out_o, qkv_o, gain_one_o, gain_two_o, rg_o = take(7)
    vm = dict(zip(BACK_IN, take(len(BACK_IN))))
    dkT, dvT, delta, dP, prior_out, prior_in, dws, g_stage, g_core, g_x, g_acc, qkv_v, wq_rows, wu_rows = take(14)
    p, hd, row = Place(n), HD, blocks * tok
    mine, width = heads * hd, blocks * heads * hd
    share, part = width // blocks, width // 2
    rows_out = lambda ref, at, count: ref.at[pl.ds(at, count)]
    per_part = part // share

    def up_outs(k):
        return [
            (pl.ds(j * share, share), up_o.at[:, pl.ds((k * per_part + j) * width, width)]) for j in range(per_part)
        ]

    plans = [
        ("d0", "share", share_d, 0, part, width, [(pl.ds(0, part), rows_out(down_o, 0, part))]),
        ("d1", "pair", pair_d, 0, part, width, [(pl.ds(0, part), rows_out(down_o, part, part))]),
    ]
    for k in range(parts // per_part):
        plans.append((("u", k), "whole", gu, k * part, part, width, up_outs(k)))
    out_parts = [(pl.ds(k * share, share), out_o.at[:, pl.ds(k * part, part)]) for k in range(2)]
    plans.append(("o", "whole", go, 0, 2 * share, part, out_parts))
    for k in range(heads):
        plans.append((("q", k), "share", None, 0, row // tok * mine, mine, []))
    bufs = [take(len(Sum.scratch(plan[1], 16, 128, n))) for plan in plans]
    sems = refs.pop(0)
    c = Copies(sems)
    for name in BACK_IN:
        src = (lambda: hbm["x"].at[:, 0, :]) if name == "x" else (lambda name=name: hbm[name])
        c.local(name, src, lambda name=name: vm[name])
    c.local("wq rows", lambda: w_qkv.at[rows_at(p.s * share, share)], lambda: wq_rows)
    c.local("wu rows", lambda: w_up.at[rows_at(p.s * share, share)], lambda: wu_rows)
    sums = [Sum(p, c, plan[0], plan[1], plan[2], plan[3], plan[4], plan[5], buf, plan[6]) for plan, buf in zip(plans, bufs)]
    d0, d1, u0, u1, o, qkv = sums[0], sums[1], sums[2], sums[3], sums[4], sums[5:]
    for k in range(heads):
        spot = lambda k=k: qkv[k].own.at[0, rows_at(p.s * mine, mine)]
        for what, mate in (("cross", p.cross_mate), ("chip", p.chip_mate), ("core", p.core_mate)):
            c.remote(("dw", k, what), lambda k=k, mate=mate: dws.at[k, rows_at(mate()[0] * mine, mine)], spot, mate)
        c.local(("dw", k, "own"), lambda k=k: dws.at[k, rows_at(p.s * mine, mine)], spot)
        c.remote(("prior", k), lambda k=k: prior_out.at[k], lambda k=k: prior_in.at[k], p.prior_row)
    for order in (1, 0):
        c.remote(("gh", order), lambda order=order: g_stage.at[order], lambda order=order: g_core.at[order], p.core_mate)
    c.remote(("gh", "x"), lambda: g_stage.at[1], lambda: g_x, p.chip_mate)
    c.local("rg", lambda: vm["gm"], lambda: rg_o.at[:, 0, :])
    c.local("qkv", lambda: qkv_v, lambda: qkv_o)

    first = BACK_IN[:8]
    c.start(*first)
    greet(p.all_mates())
    d1.p0()
    d0.p0()
    u0.p0()
    c.start(*BACK_IN[8:], "wq rows", "wu rows")
    d0.p2()
    u0.p1()
    u1.p0()
    o.p0()
    c.wait(*first)
    dqT = vm["oT"]
    doT, kk, vv, kT, qT, lse, start = (vm[x] for x in ("doT", "k", "v", "kT", "qT", "lse", "start"))

    def make_delta(h, carry):
        rows = pl.ds(pl.multiple_of(h * hd, hd), hd)
        delta[h] = jnp.sum(doT[rows, :].astype(F32) * vm["oT"][rows, :], axis=0, keepdims=True)
        return carry

    lax.fori_loop(0, heads, make_delta, 0)
    dqT[...] = jnp.zeros_like(dqT)
    dkT[...] = jnp.zeros_like(dkT)
    dvT[...] = jnp.zeros_like(dvT)

    def pair(h, q0, qw, k0, kw, causal):
        hr = pl.ds(pl.multiple_of(h * hd, hd), hd)
        qs, ks = pl.ds(pl.multiple_of(q0, 128), qw), pl.ds(pl.multiple_of(k0, 128), kw)
        q_blk, do_blk = qT[hr, qs], doT[hr, qs]
        s = dot(kk[h, ks, :], q_blk)
        e = jnp.exp(s - lse[h, :, qs])
        at = lax.broadcasted_iota(jnp.int32, s.shape, 0) + k0
        keep = at >= start[:, qs]
        if causal:
            until = lax.broadcasted_iota(jnp.int32, s.shape, 1) + (q0 + tok)
            keep = keep & (at <= until)
        e = jnp.where(keep, e, 0.0)
        dp = dot(vv[h, ks, :], do_blk)
        ds = (e * (dp - delta[h, :, qs])).astype(BF16)
        dvT[hr, ks] += dot_nt(do_blk, e.astype(BF16))
        dkT[hr, ks] += dot_nt(q_blk, ds)
        dqT[hr, qs] += dot(kT[hr, ks], ds)

    def full(h, first, last):
        def one(t, carry):
            i = jnp.where(t == 0, 0, jnp.where(t <= 3, 3, jnp.where(t <= 5, 2, 1)))
            j = jnp.where(t == 0, 0, jnp.where(t <= 3, t, jnp.where(t <= 5, t - 3, 1)))
            pair(h, i * tok, tok, j * tok, tok, False)
            return carry

        lax.fori_loop(first, last, one, 0)

    def diagonal(h):
        sub = tok // 2

        def one(i, carry):
            pair(h, i * tok, tok, (i + 1) * tok, sub, True)
            pair(h, i * tok + sub, sub, (i + 1) * tok + sub, sub, True)
            return carry

        lax.fori_loop(0, blocks, one, 0)

    def fill_prior(h):
        hr = pl.ds(pl.multiple_of(h * hd, hd), hd)
        prior_out[h, 0:hd, :] = dkT[hr, 0:tok].astype(BF16)
        prior_out[h, hd : 2 * hd, :] = dvT[hr, 0:tok].astype(BF16)

    def close(h):
        hr = pl.ds(pl.multiple_of(h * hd, hd), hd)
        last = pl.ds(row, tok)
        dkT[hr, last] += prior_in[h, 0:hd, :].astype(F32)
        dvT[hr, last] += prior_in[h, hd : 2 * hd, :].astype(F32)
        base = h * 3 * hd
        for k, (src, at) in enumerate(((dqT, 0), (dkT, tok), (dvT, tok))):
            val = src[hr, at:]
            val = val * (1.0 / math.sqrt(hd)) if k == 0 else val
            dP[pl.ds(pl.multiple_of(base + k * hd, hd), hd), :] = val.astype(BF16)
        dws[h] = dot_nt(vm["hT"][...], dP[pl.ds(pl.multiple_of(base, hd), 3 * hd), :]).astype(BF16)

    def send_dw(k):
        return lambda: c.start(*[("dw", k, what) for what in DW])

    def dw_here(k):
        return lambda: c.wait(*[("dw", k, what) for what in DW])

    def at_head(h, *todo):
        for k, steps in enumerate(todo):
            if steps:
                @pl.when(h == k)
                def _():
                    for step in steps:
                        step()

    def head(h, carry):
        full(h, 0, 1)
        fill_prior(h)
        at_head(h, *[[lambda k=k: c.start(("prior", k))] for k in range(heads)])
        full(h, 1, 4)
        at_head(h, [d0.p3, u1.p1], [d0.p6, d1.p4, u0.p2], [d1.p6, u0.p4, u1.p2])
        full(h, 4, 7)
        at_head(h, [d0.p4], [d1.p5, u0.p3], [u0.p5, u1.p3])
        diagonal(h)
        at_head(h, [d1.p2, d0.p5], [o.p1], [u0.p6])
        at_head(h, *[[lambda k=k: c.wait(("prior", k))] for k in range(heads)])
        if heads:
            at_head(h, [lambda: c.wait("hT", "wm")])
        close(h)
        at_head(h, [send_dw(0), d1.p3], [send_dw(1), dw_here(0), qkv[0].p2], [send_dw(2), dw_here(1), qkv[1].p2])
        return carry

    lax.fori_loop(0, heads, head, 0)

    def grad_h_part(owner):
        return dot(vm["wm"][...], dP[:, pl.ds(pl.multiple_of(owner * tok, tok), tok)])

    def core_grad(order):
        chip = lax.rem(p.chip + order, 2)
        g_stage[order] = grad_h_part(2 * chip + 1 - p.core).astype(BF16)
        c.start(("gh", order))

    core_grad(1)
    core_grad(0)
    g_acc[...] = grad_h_part(2 * (1 - p.chip) + p.core)
    c.wait(("gh", 1))
    g_stage[1] = (g_acc[...] + g_core[1].astype(F32)).astype(BF16)
    c.start(("gh", "x"))
    qkv[0].p3()
    u1.p4()
    g_acc[...] = grad_h_part(2 * p.chip + p.core)
    c.wait(("gh", 0))
    g_acc[...] += g_core[0].astype(F32)
    dw_here(2)()
    qkv[2].p2()
    qkv[1].p3()
    qkv[0].p4()
    o.p2()
    u1.p5()
    qkv[2].p3()
    qkv[1].p4()
    qkv[0].p5()
    o.p3()
    qkv[2].p4()
    qkv[1].p5()
    u1.p6()
    o.p4()
    qkv[2].p5()
    qkv[0].p6()
    qkv[1].p6()
    o.p5()
    c.wait("x", "gm", ("gh", "x"))
    gain_col = column(gain)
    vm["gm"][...] += norm_back(vm["x"][...], gain_col, g_acc[...] + g_x[...].astype(F32))
    c.start("rg")
    c.wait("wq rows", "wu rows")
    total = jnp.zeros((share, 1), F32)
    for k, one in enumerate((u0, u1)):
        for j in range(per_part):
            cols = slice((k * per_part + j) * width, (k * per_part + j + 1) * width)
            prod = one.res[j * share : (j + 1) * share, :].astype(F32) * wu_rows[:, cols].astype(F32)
            total = total + jnp.sum(prod, axis=1, keepdims=True)
    gain_two_o[...] = jnp.broadcast_to(total, gain_two_o.shape)
    qkv[2].p6()
    total = jnp.zeros((share, 1), F32)
    for k in range(3):
        for s in range(blocks):
            cells = [q.res[s * share : (s + 1) * share, k * hd : (k + 1) * hd] for q in qkv]
            cells = jnp.concatenate(cells, axis=1).astype(F32)
            cols = slice(k * width + s * mine, k * width + (s + 1) * mine)
            qkv_v[:, cols] = cells
            total = total + jnp.sum(cells * wq_rows[:, cols].astype(F32), axis=1, keepdims=True)
    gain_one_o[...] = jnp.broadcast_to(total, gain_one_o.shape)
    c.start("qkv")
    o.p6()
    for one in sums:
        one.p7()
    c.wait("qkv", "rg")


def back_pass(n, tok, blocks, ins, share_d, pair_d, gu, go, w_qkv, w_up, gain):
    heads = ins[1].shape[0]
    row = blocks * tok
    width = ins[8].shape[0]
    mine = heads * HD
    parts, share, part = w_up.shape[1] // width, width // blocks, width // 2
    v = lambda *s, t=BF16: pltpu.VMEM(s, t)
    o = lambda *s, t=BF16: jax.ShapeDtypeStruct(s, t)
    scratch = [v(width - 1, tok, t=F32) if name == "x" else pltpu.VMEM(a.shape, a.dtype) for name, a in zip(BACK_IN, ins)]
    scratch += [
        v(mine, row + tok, t=F32), v(mine, row + tok, t=F32), v(heads, 1, row, t=F32), v(3 * mine, row),
        v(heads, 2 * HD, tok), v(heads, 2 * HD, tok), v(heads, width, mine),
        v(2, width, tok), v(2, width, tok), v(width, tok), v(width, tok, t=F32), v(share, 3 * width, t=F32),
        v(share, 3 * width), v(share, w_up.shape[1]),
    ]
    modes = [("share", part, width), ("pair", part, width), ("whole", part, width), ("whole", part, width)]
    modes += [("whole", 2 * share, part)] + [("share", blocks * mine, mine)] * heads
    copies = len(ins) + 5 * heads + 8
    for mode, rows, cols in modes:
        scratch += Sum.scratch(mode, rows, cols, n)
        copies += 16 + n // 8
    scratch.append(pltpu.SemaphoreType.DMA((2, copies)))
    hbm = pl.BlockSpec(memory_space=pl.ANY)
    vmem = pl.BlockSpec(memory_space=pltpu.VMEM)
    return pl.pallas_call(
        functools.partial(back_kernel, n, tok, blocks, heads, parts),
        out_shape=[
            o(width, width), o(share, parts * width), o(share, width), o(share, 3 * width, t=F32),
            o(share, 128, t=F32), o(share, 128, t=F32), o(width - 1, 1, tok, t=F32),
        ],
        in_specs=[hbm] * (len(ins) + 6) + [vmem],
        out_specs=[hbm] * 4 + [vmem, vmem, hbm],
        scratch_shapes=scratch,
        compiler_params=pltpu.CompilerParams(collective_id=1, has_side_effects=True, vmem_limit_bytes=VMEM_LIMIT),
    )(*ins, share_d, pair_d, gu, go, w_qkv, w_up, gain)


def per_device(residual, documents, gain_one, gain_two, w_qkv, w_out, w_up, w_down, cotangent):
    blocks = lax.axis_size("seq")
    n = lax.axis_size("batch")
    place = lax.axis_index("seq")
    tok, width = residual.shape[1], w_out.shape[0]
    share = width // blocks
    x = jnp.transpose(residual, (2, 0, 1))
    cot = jnp.transpose(cotangent, (2, 0, 1))
    attT, hT, kT, qT, oT, lse, start, k, v, w_mine = fore_pass(n, tok, blocks, x, gain_one[None], documents, w_qkv)
    new, grad_middle, doT, grad_up, grad_out, down_share, down_pair = mid_pass(
        n, blocks, x, cot, attT, gain_two[None], w_out, w_up, w_down
    )
    sum_down, sum_up, sum_out, sum_qkv, one, two, grad_x = back_pass(
        n, tok, blocks, (doT, k, v, kT, qT, oT, lse, start, hT, w_mine, x, grad_middle),
        down_share, down_pair, grad_up, grad_out, w_qkv, w_up, gain_one[None],
    )

    def gain_grad(total, gain):
        return total[:, 0] / lax.dynamic_slice_in_dim(gain, place * share, share)

    return (
        jnp.transpose(new, (1, 2, 0)),
        jnp.transpose(grad_x, (1, 2, 0)),
        gain_grad(one, gain_one),
        gain_grad(two, gain_two),
        sum_qkv,
        sum_out.astype(F32),
        sum_up.astype(F32),
        sum_down.astype(F32),
    )


def solution(mesh):
    placed = (
        P("batch", "seq", None),
        P("batch", "seq"),
        P(),
        P(),
        P(),
        P(),
        P(),
        P(),
        P("batch", "seq", None),
    )
    return jax.shard_map(
        per_device,
        mesh=mesh,
        in_specs=placed,
        out_specs=(
            P("batch", "seq", None),
            P("batch", "seq", None),
            P("seq"),
            P("seq"),
            P("seq", None),
            P("seq", None),
            P("seq", None),
            P("seq", None),
        ),
        check_vma=False,
    )
```

profile of v0, /device:TPU:0, one launch (start us, length us, event | category | flops | bytes accessed | tf_op | source)
XLA Modules:
  0.0 236.6 jit_solution(10638951734665748122)
XLA Ops:
  0.6 1.3 broadcast_in_dim.7.refs_1_.refs_18_
  1.9 0.0 copy-start.4
  1.9 50.3 %shard_map.152 = (bf16[768,512]{1,0:T(8,128)(2,1)}, bf16[768,2048]{1,0:T(8,128)(2,1)}, bf16[192,2560]{1,0:T(8,128)(2,1)}, bf16[192,2048]{1,0:T(8,128)(2,1)}, f32...) custom-call(f32[767,1,512]{2,1,0:T(1,128)} %bitcast.4, ...), custom_call_target="tpu_custom_call" | custom-call | tf_op jit(solution)/shard_map/pallas_call | solution.py:556
  52.3 0.0 copy-done.4
  52.3 0.6 broadcast_in_dim.8.refs_3_
  52.9 36.3 %shard_map.153 = (f32[767,1,512]{2,1,0:T(1,128)}, f32[767,512]{1,0:T(8,128)}, bf16[192,2048]{1,0:T(8,128)(2,1)}, bf16[4,768,768]{2,1,0:T(8,128)(2,1)}, bf16[4,38...) custom-call(f32[767,1,512]{2,1,0:T(1,128)} %bitcast.5, f32[767,1,512]{2,1,0:T(1,128)} %bitcast.7, ...), custom_call_target="tpu_custom_call" | custom-call | tf_op jit(solution)/shard_map/pallas_call | solution.py:710
  89.2 132.2 %shard_map.154 = (bf16[768,768]{1,0:T(8,128)(2,1)}, bf16[192,3072]{1,0:T(8,128)(2,1)}, bf16[192,768]{1,0:T(8,128)(2,1)}, f32[192,2304]{1,0:T(8,128)}, f32[192,12...) custom-call(bf16[192,2048]{1,0:T(8,128)(2,1)} %get-tuple-element.34.refs_0_, ...), custom_call_target="tpu_custom_call" | custom-call | tf_op jit(solution)/shard_map/pallas_call | solution.py:980
  221.4 1.1 slice_reduce_fusion
  222.5 1.3 dynamic-slice_divide_fusion.1
  223.8 0.6 dynamic-slice_divide_fusion
  224.4 1.8 convert_element_type.9
  226.2 0.0 copy-start.3
  226.2 3.0 %convert_element_type.10 = f32[192,3072]{1,0:T(8,128)} convert(bf16[192,3072]{1,0:T(8,128)(2,1)} %get-tuple-element.54) | non-fusion elementwise | flops 589824 | bytes 3538944 | tf_op jit(solution)/shard_map/convert_element_type | solution.py:1020
  229.3 0.0 copy-done.3
  229.3 0.0 copy-start.1
  229.3 1.6 convert_element_type.11
  230.9 0.5 copy-done.1
  231.4 0.0 copy-start.2
  231.4 1.1 copy.20
  232.5 0.8 copy-done.2
  233.4 0.0 copy-start
  233.4 1.1 copy.21
  234.5 0.9 copy-done
  235.4 1.2 copy.22
Async XLA Ops:
  1.9 50.4 %copy-start.4 = (f32[768]{0:T(1024)S(1)}, f32[768]{0:T(1024)}, u32[]{:S(2)}) copy-start(f32[768]{0:T(1024)} %param.12) | copy-start | bytes 9220
  226.2 3.0 %copy-start.3 = (bf16[768,768]{1,0:T(8,128)(2,1)S(1)}, bf16[768,768]{1,0:T(8,128)(2,1)}, u32[]{:S(2)}) copy-start(bf16[768,768]{1,0:T(8,128)(2,1)} %get-tuple-element.55) | copy-start | bytes 3538948
  229.3 2.1 copy-start.1
  231.4 2.0 copy-start.2
  233.4 2.0 copy-start
where the time goes:
time: 237 us
  Pallas kernels  219 us (92%)
  local copies, waits for them, and re-layouts  8.7 us (4%)
  other arithmetic  8.39 us (4%)
    pallas_call x1, Pallas kernels, back_pass(): pl.pallas_call(functools.partial(back_kernel, n, tok, blocks, heads, part...  132 us
    pallas_call x1, Pallas kernels, fore_pass(): pl.pallas_call(functools.partial(fore_kernel, n, tok, blocks, heads), out...  50.3 us
    pallas_call x1, Pallas kernels, mid_pass(): pl.pallas_call(functools.partial(mid_kernel, n, blocks), out_shape=[o(wid...  36.3 us
    unnamed x13, local copies, waits for them, and re-layouts  5.77 us

commit v1 on v0

v1 whole, which is shorter than its diff:
```python
import functools
import math

import jax
import jax.numpy as jnp
from jax import lax
from jax.experimental import pallas as pl
from jax.experimental.pallas import tpu as pltpu
from jax.sharding import PartitionSpec as P

H = 12
HD = 64
EPSILON = 1e-06
NEG = -1e30
F32, BF16 = jnp.float32, jnp.bfloat16
VMEM_LIMIT = 62 * 2**20


def dot(a, b):
    return lax.dot_general(a, b, (((1,), (0,)), ((), ())), preferred_element_type=F32)


def dot_nt(a, b):
    return lax.dot_general(a, b, (((1,), (1,)), ((), ())), preferred_element_type=F32)


def dot_tn(a, b):
    return lax.dot_general(a, b, (((0,), (0,)), ((), ())), preferred_element_type=F32)


def expand(narrow):
    return jnp.concatenate([narrow, -jnp.sum(narrow, axis=0, keepdims=True)], axis=0)


def shrink(full_vec):
    return full_vec[:-1] - jnp.mean(full_vec, axis=0, keepdims=True)


def shrink_back(grad_narrow):
    padded = jnp.concatenate([grad_narrow, jnp.zeros_like(grad_narrow[:1])], axis=0)
    return padded - jnp.sum(grad_narrow, axis=0, keepdims=True) / padded.shape[0]


def root(full_vec):
    return lax.rsqrt(jnp.mean(full_vec * full_vec, axis=0, keepdims=True) + EPSILON)


def norm_back(narrow, gain, grad_h):
    full_vec = expand(narrow)
    r = root(full_vec)
    scaled = gain * grad_h
    grad_full = r * (scaled - full_vec * (r * r * jnp.mean(scaled * full_vec, axis=0, keepdims=True)))
    return grad_full[:-1] - grad_full[-1:]


def column(gain_ref):
    return jnp.broadcast_to(gain_ref[...].reshape(1, gain_ref.shape[0]), (8, gain_ref.shape[0])).T[:, 0:1]


MESH = pl.DeviceIdType.MESH


class Place:
    def __init__(self, n):
        self.s = lax.axis_index("seq")
        self.b = lax.axis_index("batch")
        self.core = lax.rem(self.s, 2)
        self.chip = self.s // 2
        self.y = lax.rem(self.b, 2)
        self.z = lax.rem(self.b // 2, 4)
        self.far = self.b // 8
        self.n = n

    def core_mate(self):
        return (self.s + 1 - 2 * self.core, self.b)

    def chip_mate(self):
        return (self.s + 2 - 4 * self.chip, self.b)

    def cross_mate(self):
        return (3 - self.s, self.b)

    def y_mate(self):
        return (self.s, self.b + 1 - 2 * self.y)

    def z_of(self, d):
        return lax.rem(self.z + d, 4)

    def z_mate(self, d):
        return (self.s, self.b + 2 * (self.z_of(d) - self.z))

    def z_pair(self, bit):
        here = lax.rem(self.z // bit, 2)
        return (self.s, self.b + 2 * bit * (1 - 2 * here))

    def far_mate(self, d):
        f = lax.rem(self.far + d, self.n // 8)
        return (self.s, self.b + 8 * (f - self.far))

    def next_row(self):
        return (self.s, lax.rem(self.b + 1, self.n))

    def prior_row(self):
        return (self.s, lax.rem(self.b + self.n - 1, self.n))

    def all_mates(self):
        mates = [self.core_mate(), self.chip_mate(), self.cross_mate(), self.y_mate()]
        mates += [self.z_mate(d) for d in (1, 2, 3)]
        mates += [self.far_mate(d) for d in range(1, self.n // 8)]
        return mates + [self.next_row(), self.prior_row()]


def greet(mates):
    barrier = pltpu.get_barrier_semaphore()
    for mate in mates:
        pl.semaphore_signal(barrier, inc=1, device_id=mate, device_id_type=MESH)
    pl.semaphore_wait(barrier, len(mates))


class Copies:
    def __init__(self, sems):
        self.sems, self.made = sems, {}

    def remote(self, name, src, dst, mate):
        k = len(self.made)

        def make():
            return pltpu.make_async_remote_copy(
                src_ref=src(),
                dst_ref=dst(),
                send_sem=self.sems.at[0, k],
                recv_sem=self.sems.at[1, k],
                device_id=mate(),
                device_id_type=MESH,
            )

        assert name not in self.made
        self.made[name] = make

    def local(self, name, src, dst):
        k = len(self.made)

        def make():
            return pltpu.make_async_copy(src(), dst(), self.sems.at[0, k])

        assert name not in self.made
        self.made[name] = make

    def start(self, *names):
        for name in names:
            self.made[name]().start()

    def wait(self, *names):
        for name in names:
            self.made[name]().wait()

    def wait_recv(self, *names):
        for name in names:
            self.made[name]().wait_recv()

    def wait_send(self, *names):
        for name in names:
            self.made[name]().wait_send()


def rows_at(at, count):
    return pl.ds(pl.multiple_of(at, 16), count)


def blockwise(rows, body):
    step = next(s for s in (48, 32, 16) if rows % s == 0)

    def one(i, carry):
        body(i * step, step)
        return carry

    lax.fori_loop(0, rows // step, one, 0)


class Sum:
    def __init__(self, place, copies, name, mode, far_z, src, first, rows, cols, bufs, out):
        self.p, self.c, self.name, self.mode, self.far_z = place, copies, name, mode, far_z
        self.src, self.first, self.rows, self.cols, self.out = src, first, rows, cols, out
        bufs = list(bufs)
        self.full = bufs.pop(0) if out else None
        self.own, self.ry, self.rz, self.res, self.rf = bufs[:5]
        self.rc = bufs[5] if mode in "xy" else None
        self.rx = bufs[-1] if mode != "share" else None
        self.mine = (lambda: self.own.at[self.p.chip]) if mode in "xy" else (lambda: self.own.at[0])
        self.define()

    @staticmethod
    def scratch(mode, far_z, rows, cols, n, full):
        def v(*s):
            return pltpu.VMEM(s, BF16)

        half, spot = rows // 2, rows // (8 if far_z else 4)
        out = [v(2 if mode in "xy" else 1, rows, cols), v(2 if mode == "y" else 1, half, cols)]
        out += [v(3 if far_z else 2, spot, cols), v(rows, cols), v(n // 8 if n > 8 else 1, spot if n > 8 else 16, cols)]
        if mode in "xy":
            out.append(v(2, rows, cols))
        if mode != "share":
            out.append(v(rows if mode == "x" else half, cols))
        return [pltpu.VMEM((rows, cols), F32)] + out if full else out

    def id(self, what):
        return (self.name, what)

    def at_half(self, y):
        return rows_at(y * (self.rows // 2), self.rows // 2)

    def at_spot(self):
        p, half = self.p, self.rows // 2
        if self.far_z:
            return rows_at(p.y * half + p.z * (half // 4), half // 4)
        return rows_at(p.y * half + lax.rem(p.z, 2) * (half // 2), half // 2)

    def define(self):
        p, c, half, far = self.p, self.c, self.rows // 2, self.p.n // 8
        if self.mode in "xy":
            first = pl.ds(self.first, self.rows)
            for order in (1, 0):
                chip = lambda order=order: lax.rem(p.chip + order, 2)
                c.remote(
                    self.id(("core", order)),
                    lambda chip=chip: self.src.at[2 * chip() + 1 - p.core, first],
                    lambda chip=chip: self.rc.at[chip()],
                    p.core_mate,
                )
                c.local(
                    self.id(("own", order)),
                    lambda chip=chip: self.src.at[2 * chip() + p.core, first],
                    lambda chip=chip: self.own.at[chip()],
                )
        other = lambda: self.own.at[1 - p.chip]
        if self.mode == "x":
            c.remote(self.id("x"), other, lambda: self.rx, p.chip_mate)
        if self.mode == "y":
            c.remote(self.id("y1"), lambda: other().at[self.at_half(1 - p.y)], lambda: self.ry.at[1], p.y_mate)
            c.remote(self.id("x"), lambda: other().at[self.at_half(p.y)], lambda: self.rx, p.chip_mate)
        if self.mode == "share" and self.src is not None:
            c.local(self.id("own"), lambda: self.src, lambda: self.own.at[0])
        if self.mode == "half":
            c.remote(self.id("x"), lambda: self.src.at[1 - p.chip], lambda: self.rx, p.chip_mate)
            c.local(self.id("own"), lambda: self.src.at[p.chip], lambda: self.own.at[0, self.at_half(p.y)])
        else:
            c.remote(self.id("y"), lambda: self.mine().at[self.at_half(1 - p.y)], lambda: self.ry.at[0], p.y_mate)
        spot = lambda: self.res.at[self.at_spot()]
        if self.far_z:
            for d in (2, 1, 3):
                c.remote(
                    self.id(("z", d)),
                    lambda d=d: self.mine().at[rows_at(p.y * half + p.z_of(d) * (half // 4), half // 4)],
                    lambda d=d: self.rz.at[3 - d],
                    lambda d=d: p.z_mate(d),
                )
                c.remote(self.id(("back z", d)), spot, spot, lambda d=d: p.z_mate(d))
        else:
            away = lambda: rows_at(p.y * half + (1 - lax.rem(p.z, 2)) * (half // 2), half // 2)
            c.remote(self.id("z1"), lambda: self.mine().at[away()], lambda: self.rz.at[0], lambda: p.z_pair(1))
            c.remote(self.id("z2"), lambda: self.mine().at[self.at_spot()], lambda: self.rz.at[1], lambda: p.z_pair(2))
            c.remote(self.id("back z1"), spot, spot, lambda: p.z_pair(1))
        for d in range(1, far):
            c.remote(self.id(("far", d)), lambda: self.rf.at[p.far], lambda: self.rf.at[p.far], lambda d=d: p.far_mate(d))
        my_half = lambda: self.res.at[self.at_half(p.y)]
        c.remote(self.id("back y"), my_half, my_half, p.y_mate)
        for k, (src, dst) in enumerate(self.out):
            c.local(self.id(("out", k)), lambda src=src: self.full.at[src], lambda dst=dst: dst)

    def add(self, dst, at, rows, *others):
        def body(first, step):
            here = rows_at(at + first, step)
            total = dst[here, :].astype(F32)
            for other, offset in others:
                total = total + other[rows_at(offset + first, step), :].astype(F32)
            dst[here, :] = total.astype(BF16)

        blockwise(rows, body)

    def p0(self):
        if self.mode == "half":
            self.c.start(self.id("x"), self.id("own"))
        if self.mode == "share":
            self.c.start(self.id("own"))
        if self.mode in "xy":
            for order in (1, 0):
                self.c.start(self.id(("core", order)), self.id(("own", order)))

    def p1(self):
        self.c.wait(self.id(("core", 1)), self.id(("own", 1)))
        other = 1 - self.p.chip
        self.add(self.own.at[other], 0, self.rows, (self.rc.at[other], 0))
        self.c.start(self.id("x" if self.mode == "x" else "y1"))

    def p1b(self):
        self.c.wait(self.id(("core", 0)), self.id(("own", 0)))
        self.add(self.mine(), 0, self.rows, (self.rc.at[self.p.chip], 0))
        if self.mode == "y":
            self.c.start(self.id("y"))

    def p2(self):
        p, half = self.p, self.rows // 2
        if self.mode == "y":
            self.c.wait(self.id("y1"))
            self.add(self.own.at[1 - p.chip], p.y * half, half, (self.ry.at[1], 0))
            self.c.start(self.id("x"))
            return
        if self.mode == "x":
            self.c.wait(self.id("x"))
            self.add(self.mine(), (1 - p.y) * half, half, (self.rx, (1 - p.y) * half))
        if self.mode == "share" and self.src is not None:
            self.c.wait(self.id("own"))
        self.c.start(self.id("y"))

    def p3(self):
        p, half, more = self.p, self.rows // 2, []
        if self.mode != "half":
            self.c.wait(self.id("y"))
            more.append((self.ry.at[0], 0))
        if self.mode == "x":
            more.append((self.rx, p.y * half))
        if self.mode in ("y", "half"):
            self.c.wait(self.id("x"))
            more.append((self.rx, 0))
        if self.mode == "half":
            self.c.wait(self.id("own"))
        self.add(self.mine(), p.y * half, half, *more)
        self.c.start(*([self.id(("z", d)) for d in (2, 1, 3)] if self.far_z else [self.id("z1")]))

    def total(self, *others):
        p = self.p
        spot, rows = self.at_spot(), self.at_spot().size
        own, far = self.mine(), p.n // 8

        def body(first, step):
            here = rows_at(spot.start + first, step)
            there = rows_at(first, step)
            total = own[here, :].astype(F32)
            for other in others:
                total = total + other[there, :].astype(F32)
            if far > 1:
                self.rf[p.far, there, :] = total.astype(BF16)
            else:
                self.res[here, :] = total.astype(BF16)

        blockwise(rows, body)
        if far > 1:
            self.c.start(*[self.id(("far", d)) for d in range(1, far)])
            self.c.wait(*[self.id(("far", d)) for d in range(1, far)])

            def more(first, step):
                there = rows_at(first, step)
                total = self.rf[0, there, :].astype(F32)
                for k in range(1, far):
                    total = total + self.rf[k, there, :].astype(F32)
                self.res[rows_at(spot.start + first, step), :] = total.astype(BF16)

            blockwise(rows, more)

    def p4(self):
        if self.far_z:
            self.c.wait(*[self.id(("z", d)) for d in (1, 2, 3)])
            self.total(*[self.rz.at[d] for d in range(3)])
            self.c.start(*[self.id(("back z", d)) for d in (2, 1, 3)])
            return
        self.c.wait(self.id("z1"))
        spot = self.at_spot()
        self.add(self.mine(), spot.start, spot.size, (self.rz.at[0], 0))
        self.c.start(self.id("z2"))

    def p4b(self):
        if not self.far_z:
            self.c.wait(self.id("z2"))
            self.total(self.rz.at[1])
            self.c.start(self.id("back z1"))

    def p5(self):
        self.c.wait(*([self.id(("back z", d)) for d in (1, 2, 3)] if self.far_z else [self.id("back z1")]))
        self.c.start(self.id("back y"))

    def p6(self):
        self.c.wait(self.id("back y"))
        if not self.out:
            return

        def body(first, step):
            here = rows_at(first, step)
            self.full[here, :] = self.res[here, :].astype(F32)

        blockwise(self.rows, body)
        self.c.start(*[self.id(("out", k)) for k in range(len(self.out))])

    def p7(self):
        self.c.wait(*[self.id(("out", k)) for k in range(len(self.out))])


def fore_kernel(n, tok, blocks, heads, *refs):
    x, gain, docs, w = refs[:4]
    attT_o, hT_o, kT_o, qT_o, oT_o, lse_o, start_o, k_o, v_o, wm_o = refs[4:14]
    xs, ws, wm, hT, docs_all, prior_docs, start, kT, vT, qT, kk, vv, acc, m_ref, l_ref, lse, stage, sems = refs[14:]
    width = xs.shape[0] + 1
    row = blocks * tok
    mine = heads * HD
    p = Place(n)
    c = Copies(sems)
    mates = {"core": p.core_mate, "chip": p.chip_mate, "cross": p.cross_mate}
    block = lambda at: pl.ds(pl.multiple_of(at * tok, tok), tok)
    here = lambda: block(p.s)
    c.local("x", lambda: x.at[:, 0, :], lambda: xs)
    c.local("w", lambda: w, lambda: ws)
    c.local("docs", lambda: docs, lambda: docs_all.at[:, here()])
    for name, mate in mates.items():
        c.remote(("docs", name), lambda: docs, lambda: docs_all.at[:, here()], mate)
    last = pl.ds(row - tok, tok)
    c.remote("prior docs", lambda: docs_all.at[:, last], lambda: prior_docs, p.next_row)
    c.remote("h core", lambda: hT.at[:, here()], lambda: hT.at[:, here()], p.core_mate)
    half = tok // 2
    for k in range(2):
        piece = lambda s, k=k: hT.at[:, pl.ds(pl.multiple_of(s * tok + k * half, half), half)]
        c.remote(("h chip", k), lambda piece=piece: piece(p.s), lambda piece=piece: piece(p.s), p.chip_mate)
        other = lambda piece=piece: piece(p.chip_mate()[0])
        c.remote(("h on", k), other, other, p.core_mate)
    end = pl.ds(row, tok)
    c.remote("prior k", lambda: kT.at[:, end], lambda: kT.at[:, 0:tok], p.next_row)
    c.remote("prior v", lambda: vT.at[:, end], lambda: vT.at[:, 0:tok], p.next_row)
    for h in range(heads):
        spot = lambda h=h: attT_o.at[pl.ds(pl.multiple_of(p.s * mine + h * HD, HD), HD)]
        for name, mate in mates.items():
            src = lambda h=h, mate=mate: stage.at[pl.ds(h * HD, HD), block(mate()[0])]
            c.remote(("att", h, name), src, spot, mate)
        c.local(("att", h, "own"), lambda h=h: stage.at[pl.ds(h * HD, HD), here()], spot)
    outs = {"hT": (hT, hT_o), "kT": (kT, kT_o), "qT": (qT, qT_o), "oT": (acc, oT_o), "lse": (lse, lse_o)}
    outs.update({"start": (start, start_o), "k": (kk, k_o), "v": (vv, v_o), "wm": (wm, wm_o)})
    for name, (src, dst) in outs.items():
        c.local(("out", name), lambda src=src: src, lambda dst=dst: dst)

    c.start("x", "docs", "w")
    greet([p.core_mate(), p.chip_mate(), p.cross_mate(), p.next_row(), p.prior_row()])
    c.start(*[("docs", name) for name in mates])
    c.wait("x")
    full_vec = expand(xs[...])
    hT[:, here()] = (column(gain) * full_vec * root(full_vec)).astype(BF16)
    c.start(("h chip", 0), "h core")
    c.start(("h chip", 1))

    c.wait("w")
    for s in range(blocks):
        @pl.when(p.s == s)
        def _():
            for h in range(heads):
                for k in range(3):
                    at = k * width + s * mine + h * HD
                    to = (h * 3 + k) * HD
                    wm[:, to : to + HD] = ws[:, at : at + HD]

    c.wait("docs", *[("docs", name) for name in mates])
    c.start("prior docs")
    ids = jnp.broadcast_to(docs_all[...], (8, row))
    pos = lax.broadcasted_iota(jnp.int32, (8, row), 1)
    since = jnp.where((ids != pltpu.roll(ids, 1, 1)) | (pos == 0), pos, 0)
    hop = 1
    while hop < row:
        since = jnp.maximum(since, jnp.where(pos >= hop, pltpu.roll(since, hop, 1), 0))
        hop *= 2
    start[...] = since[0:1] + tok
    m_ref[...] = jnp.full(m_ref.shape, NEG, F32)
    l_ref[...] = jnp.zeros(l_ref.shape, F32)
    acc[...] = jnp.zeros(acc.shape, F32)

    def natural(keys_at):
        keys = pl.ds(pl.multiple_of(keys_at, tok), tok)
        for h in range(heads):
            kk[h, keys, :] = kT[h * HD : (h + 1) * HD, keys].T
            vv[h, keys, :] = vT[h * HD : (h + 1) * HD, keys].T

    def project(at):
        packed = dot_tn(wm[...], hT[:, block(at)]).astype(BF16)
        keys = pl.ds(pl.multiple_of((at + 1) * tok, tok), tok)
        for h in range(heads):
            to, base = slice(h * HD, (h + 1) * HD), h * 3 * HD
            qT[to, block(at)] = packed[base : base + HD] * jnp.bfloat16(1.0 / math.sqrt(HD))
            kT[to, keys] = packed[base + HD : base + 2 * HD]
            vT[to, keys] = packed[base + 2 * HD : base + 3 * HD]
        natural((at + 1) * tok)

    def pair(h, i, j, size, causal):
        hr = pl.ds(pl.multiple_of(h * HD, HD), HD)
        qs, ks = (pl.ds(pl.multiple_of(at * tok, tok), size) for at in (i, j))
        s = dot(kk[h, ks, :], qT[hr, qs])
        at = lax.broadcasted_iota(jnp.int32, s.shape, 0)
        keep = at >= start[:, qs] - j * tok
        if causal:
            keep = keep & (at <= lax.broadcasted_iota(jnp.int32, s.shape, 1))
        s = jnp.where(keep, s, NEG)
        m = m_ref[h, :, qs]
        new_m = jnp.maximum(m, jnp.max(s, axis=0, keepdims=True))
        e = jnp.exp(s - new_m)
        shift = jnp.exp(m - new_m)
        m_ref[h, :, qs] = new_m
        l_ref[h, :, qs] = l_ref[h, :, qs] * shift + jnp.sum(e, axis=0, keepdims=True)
        acc[hr, qs] = acc[hr, qs] * shift + dot(vT[hr, ks], e.astype(BF16))

    def finish(h, i):
        hr, qs = pl.ds(pl.multiple_of(h * HD, HD), HD), block(i)
        out = acc[hr, qs] / l_ref[h, :, qs]
        acc[hr, qs] = out
        stage[hr, qs] = out.astype(BF16)
        lse[h, :, qs] = m_ref[h, :, qs] + jnp.log(l_ref[h, :, qs])

    def send_att(h, zero):
        for name, mate in list(mates.items()) + [("own", lambda: (p.s,))]:
            @pl.when((mate()[0] == 0) == zero)
            def _():
                c.start(("att", h, name))

    near, far = 2 * p.chip, 2 * (1 - p.chip)
    c.wait_recv("h core")

    def project_near(t, carry):
        project(near + t)
        return carry

    lax.fori_loop(0, 2, project_near, 0)

    @pl.when(p.chip == 1)
    def _():
        c.start("prior k", "prior v")

    def first(h, carry):
        pair(h, near, near + 1, 2 * tok, True)
        return carry

    lax.fori_loop(0, heads, first, 0)
    for k in range(2):
        c.wait_recv(("h chip", k))
        c.start(("h on", k))
    project(p.chip_mate()[0])
    c.wait_recv(("h on", 0), ("h on", 1))
    project(p.cross_mate()[0])

    @pl.when(p.chip == 0)
    def _():
        c.start("prior k", "prior v")

    def second(h, carry):
        pair(h, far, far + 1, 2 * tok, True)
        pair(h, 2, 1, 2 * tok, False)
        lax.fori_loop(1, blocks, lambda i, carry: (finish(h, i), carry)[1], 0)
        for k in range(heads):
            @pl.when(h == k)
            def _():
                send_att(k, False)
        return carry

    lax.fori_loop(0, heads, second, 0)
    c.wait_recv("prior docs")
    from_doc = docs_all[:, 0:1]
    at = lax.broadcasted_iota(jnp.int32, (1, tok), 1)
    run = jnp.max(jnp.where(prior_docs[...] != from_doc, at + 1, 0), axis=1, keepdims=True)
    start[:, 0:tok] = jnp.where(start[:, 0:tok] == tok, run, start[:, 0:tok])
    c.wait_recv("prior k", "prior v")
    natural(0)

    def third(h, carry):
        pair(h, 0, 0, tok, False)
        finish(h, 0)
        for k in range(heads):
            @pl.when(h == k)
            def _():
                send_att(k, True)
        return carry

    lax.fori_loop(0, heads, third, 0)
    c.start(*[("out", name) for name in outs])
    c.wait_send("h core", ("h chip", 0), ("h chip", 1), ("h on", 0), ("h on", 1), "prior docs", "prior k", "prior v")
    for h in range(heads):
        c.wait(*[("att", h, name) for name in list(mates) + ["own"]])
    c.wait(*[("out", name) for name in outs])


def fore_pass(n, tok, blocks, x, gain, docs, w):
    width, heads = w.shape[0], H // blocks
    row, mine = blocks * tok, heads * HD
    v = lambda *s, t=BF16: pltpu.VMEM(s, t)
    o = lambda *s, t=BF16: jax.ShapeDtypeStruct(s, t)
    hbm = pl.BlockSpec(memory_space=pl.ANY)
    scratch = [
        v(width - 1, tok, t=F32), v(width, 3 * width), v(width, 3 * mine), v(width, row),
        v(1, row, t=jnp.int32), v(1, tok, t=jnp.int32), v(1, row, t=jnp.int32),
        v(mine, row + tok), v(mine, row + tok), v(mine, row), v(heads, row + tok, HD), v(heads, row + tok, HD),
        v(mine, row, t=F32), v(heads, 1, row, t=F32), v(heads, 1, row, t=F32), v(heads, 1, row, t=F32), v(mine, row),
        pltpu.SemaphoreType.DMA((2, 24 + 4 * heads)),
    ]
    return pl.pallas_call(
        functools.partial(fore_kernel, n, tok, blocks, heads),
        out_shape=[
            o(width, tok), o(width, row), o(mine, row + tok), o(mine, row), o(mine, row, t=F32), o(heads, 1, row, t=F32),
            o(1, row, t=jnp.int32), o(heads, row + tok, HD), o(heads, row + tok, HD), o(width, 3 * mine),
        ],
        in_specs=[hbm, pl.BlockSpec(memory_space=pltpu.VMEM), hbm, hbm],
        out_specs=[hbm] * 10,
        scratch_shapes=scratch,
        compiler_params=pltpu.CompilerParams(collective_id=0, has_side_effects=True, vmem_limit_bytes=VMEM_LIMIT),
    )(x, gain, docs, w)


def gelu_both(v, grad):
    rate = math.sqrt(2.0 / math.pi)
    square = v * v
    th = jnp.tanh(rate * v * (1.0 + 0.044715 * square))
    up = 0.5 * (1.0 + th)
    slope = up + 0.5 * v * (1.0 - th * th) * (rate * (1.0 + 3.0 * 0.044715 * square))
    return (v * up).astype(BF16), (grad * slope).astype(BF16)


def mid_kernel(n, blocks, *refs):
    x, cot, attT, gain, w_out, w_up, w_down = refs[:7]
    new_o, gm_o, doT_o, gu_o, go_o, half_o, share_o = refs[7:14]
    xs, cs, at, wo, wu, wd, mid, h2, g2, g1, geluT, gupT, b2, gh, dw, rc, ry, rx, ga, gu, go, sems = refs[14:]
    tok, width = xs.shape[1], xs.shape[0] + 1
    parts = wu.shape[1] // width
    share = width // blocks
    p = Place(n)
    c = Copies(sems)
    mates = {"cross": p.cross_mate, "chip": p.chip_mate, "core": p.core_mate}
    c.local("att", lambda: attT, lambda: at)
    c.local("wo", lambda: w_out, lambda: wo)
    c.local("x", lambda: x.at[:, 0, :], lambda: xs)
    c.local("cot", lambda: cot.at[:, 0, :], lambda: cs)
    c.local("wu", lambda: w_up, lambda: wu)
    c.local("wd", lambda: w_down, lambda: wd)
    c.remote("core 0", lambda: dw.at[0], lambda: rc.at[0], p.core_mate)
    c.remote("core 1", lambda: dw.at[2], lambda: rc.at[1], p.core_mate)
    part = width // 2
    fourth = part // 2
    low = lambda y: rows_at(y * fourth, fourth)
    for t in range(2):
        c.remote(("y", t), lambda t=t: dw.at[2 * t + 1, low(1 - p.y)], lambda t=t: ry.at[t], p.y_mate)
        dst = lambda t=t: half_o.at[1 - p.chip if t == 0 else p.chip]
        c.local(("half", t), lambda t=t: dw.at[2 * t + 1, low(p.y)], dst)
    high = pl.ds(part, part)
    c.remote("chip", lambda: dw.at[1, high], lambda: rx, p.chip_mate)
    c.local("share", lambda: dw.at[3, high], lambda: share_o)
    there = lambda: doT_o.at[:, pl.ds(pl.multiple_of(p.s * tok, tok), tok)]
    for name, mate in mates.items():
        c.remote(("ga", name), lambda mate=mate: ga.at[rows_at(mate()[0] * share, share)], there, mate)
    c.local(("ga", "own"), lambda: ga.at[rows_at(p.s * share, share)], there)
    c.local("new out", lambda: xs, lambda: new_o.at[:, 0, :])
    c.local("gm", lambda: cs, lambda: gm_o)
    for k in range(parts):
        c.local(("gu", k), lambda k=k: gu.at[:, pl.ds(k * share, share)], lambda k=k: gu_o.at[:, pl.ds(k * share, share)])
    c.local("go", lambda: go, lambda: go_o)

    c.start("att", "wo", "x", "cot", "wu", "wd")
    greet([p.core_mate(), p.chip_mate(), p.cross_mate(), p.y_mate()])
    c.wait("att", "wo")
    branch_one = dot_tn(wo[...], at[...])
    c.wait("x")
    mid[...] = xs[...] + shrink(branch_one)
    full_vec = expand(mid[...])
    gain_col = column(gain)
    h2[...] = (gain_col * full_vec * root(full_vec)).astype(BF16)
    c.wait("cot")
    g2[...] = shrink_back(cs[...]).astype(BF16)
    b2[...] = jnp.zeros_like(b2)
    gh[...] = jnp.zeros_like(gh)
    c.wait("wu", "wd")

    def add(dst, at, src, rows):
        def body(first, step):
            r = rows_at(at + first, step)
            dw[dst, r, :] = (dw[dst, r, :].astype(F32) + src[rows_at(first, step), :].astype(F32)).astype(BF16)

        blockwise(rows, body)

    def chip_sum(t):
        c.wait_recv(f"core {t}")
        add(2 * t + 1, 0, rc.at[t], width)
        c.start(("y", t), *(["chip"] if t == 0 else []))

    def y_sum(t):
        c.wait(("y", t))
        add(2 * t + 1, p.y * fourth, ry.at[t], fourth)
        c.start(("half", t))

    def piece(t, carry):
        s = jnp.where(t == 0, p.cross_mate()[0], jnp.where(t == 1, p.chip_mate()[0], jnp.where(t == 2, p.core_mate()[0], p.s)))
        its = pl.ds(pl.multiple_of(s * width, width), width)
        up = dot_tn(wu[:, its], h2[...])
        grad_gelu = dot(wd[its, :], g2[...])
        gelu, grad_up = gelu_both(up, grad_gelu)
        geluT[...] = gelu
        gupT[its, :] = grad_up
        dw[t] = dot_nt(geluT[...], g2[...]).astype(BF16)

        @pl.when(t == 0)
        def _():
            c.start("core 0")

        @pl.when(t == 2)
        def _():
            c.start("core 1")

        b2[...] += dot_tn(wd[its, :], geluT[...])
        gh[...] += dot(wu[:, its], gupT[its, :])

        @pl.when(t == 1)
        def _():
            chip_sum(0)

        return carry

    lax.fori_loop(0, parts, piece, 0)
    chip_sum(1)
    grad_middle = cs[...] + norm_back(mid[...], gain_col, gh[...])
    cs[...] = grad_middle
    g1[...] = shrink_back(grad_middle).astype(BF16)
    ga[...] = dot(wo[...], g1[...]).astype(BF16)
    c.start(*[("ga", name) for name in list(mates) + ["own"]])
    c.start("gm")
    xs[...] = mid[...] + shrink(b2[...])
    c.start("new out")

    def up_grad(k, carry):
        its = pl.ds(pl.multiple_of(k * width, width), width)
        grad = dot_nt(h2[...], gupT[its, :]).astype(BF16)
        for s in range(blocks):
            gu[s, rows_at(k * share, share), :] = grad[s * share : (s + 1) * share]
        return carry

    lax.fori_loop(0, parts, up_grad, 0)
    c.start(*[("gu", k) for k in range(parts)])
    out_grad = dot_nt(at[...], g1[...]).astype(BF16)
    for s in range(blocks):
        for k in range(2):
            go[s, k * share : (k + 1) * share, :] = out_grad[s * share : (s + 1) * share, k * part : (k + 1) * part]
    c.start("go")
    c.wait("chip")
    add(3, part, rx, part)
    c.start("share")
    y_sum(0)
    y_sum(1)
    c.wait_send("core 0", "core 1")
    c.wait(*[("ga", name) for name in list(mates) + ["own"]])
    c.wait("gm", "new out", "go", "share", ("half", 0), ("half", 1), *[("gu", k) for k in range(parts)])


def mid_pass(n, blocks, x, cot, attT, gain, w_out, w_up, w_down):
    width, tok = attT.shape
    parts, share = w_up.shape[1] // width, width // blocks
    v = lambda *s, t=BF16: pltpu.VMEM(s, t)
    o = lambda *s, t=BF16: jax.ShapeDtypeStruct(s, t)
    hbm = pl.BlockSpec(memory_space=pl.ANY)
    scratch = [
        v(width - 1, tok, t=F32), v(width - 1, tok, t=F32), v(width, tok), v(width, width), v(*w_up.shape), v(*w_down.shape),
        v(width - 1, tok, t=F32), v(width, tok), v(width, tok), v(width, tok), v(width, tok), v(w_up.shape[1], tok),
        v(width, tok, t=F32), v(width, tok, t=F32), v(4, width, width), v(2, width, width), v(2, width // 4, width), v(width // 2, width),
        v(width, tok), v(blocks, parts * share, width), v(blocks, 2 * share, width // 2),
        pltpu.SemaphoreType.DMA((2, 32)),
    ]
    return pl.pallas_call(
        functools.partial(mid_kernel, n, blocks),
        out_shape=[
            o(width - 1, 1, tok, t=F32), o(width - 1, tok, t=F32), o(share, blocks * tok), o(blocks, parts * share, width),
            o(blocks, 2 * share, width // 2), o(2, width // 4, width), o(width // 2, width),
        ],
        in_specs=[hbm, hbm, hbm, pl.BlockSpec(memory_space=pltpu.VMEM), hbm, hbm, hbm],
        out_specs=[hbm] * 7,
        scratch_shapes=scratch,
        compiler_params=pltpu.CompilerParams(collective_id=2, has_side_effects=True, vmem_limit_bytes=VMEM_LIMIT),
    )(x, cot, attT, gain, w_out, w_up, w_down)


BACK_IN = ("doT", "k", "v", "kT", "qT", "oT", "lse", "start", "hT", "wm", "x", "gm")
DW = ("cross", "chip", "core", "own")
Q_HEADS = ((0, 1), (2,))
U_MODES = ("x", "x")
O_MODE = "y"
FAR_Z = {"d": True, "u": False, "o": False, "q": False}
PLAN = {
    "start": {
        (): ["d0.p0", "u1.p0", "u0.p0", "d1.p0", "o.p0"],
    },
    "ready": {
        (): ["u1.p1", "d1.p2"],
    },
    "prior": {
        (0,): ["u1.p1b", "u0.p1"],
        (1,): ["u0.p1b", "o.p1", "d0.p3", "o.p1b"],
    },
    "full": {
        (0, 1): ["d1.p3"],
        (1, 2): ["d0.p4"],
        (2, 2): ["o.p3"],
        (2, 5): ["d0.p5"],
    },
    "close": {
        (0,): ["u1.p2", "o.p2"],
        (1,): ["dw0", "u1.p3", "d1.p4", "u0.p2"],
        (2,): ["dw1", "gh1", "gh0", "o.p4", "d0.p6", "d1.p5", "ghA"],
    },
    "diagonal": {
        (2, 1): ["u1.p4"],
        (2, 2): ["u0.p3"],
        (2, 3): ["q0.p2"],
    },
    "end": {
        (): ["ghx", "ghB", "q1.p2", "ghC", "u1.p4b", "u0.p4", "q0.p3", "o.p4b", "u1.p5", "d1.p6", "q0.p4", "u0.p4b", "q1.p3", "o.p5", "final", "u1.p6", "q0.p4b", "u0.p5", "o.p6", "q1.p4", "q0.p5", "u0.p6", "q1.p4b", "q1.p5", "q0.p6", "q1.p6"],
    },
}


def back_sums(n, width, share, part, mine):
    half = [("d%d" % k, ("half", "share")[k], n > 8 or FAR_Z["d"], k, 0, part, width) for k in range(2)]
    up = [("u%d" % k, U_MODES[k], n > 8 or FAR_Z["u"], 0, k * part, part, width) for k in range(2)]
    out = [("o", O_MODE, n > 8 or FAR_Z["o"], 1, 0, 2 * share, part)]
    return half + up + out + [
        ("q%d" % k, "share", n > 8 or FAR_Z["q"], None, 0, width // share * mine, mine * len(hs)) for k, hs in enumerate(Q_HEADS)
    ]


def back_kernel(n, tok, blocks, heads, parts, *refs):
    refs = list(refs)
    take = lambda count: [refs.pop(0) for _ in range(count)]
    hbm = dict(zip(BACK_IN, take(len(BACK_IN))))
    down_half, down_share, gu, go, w_qkv, w_up, gain_one, gain_two = take(8)
    down_o, up_o, out_o, qkv_o, gain_one_o, gain_two_o, rg_o = take(7)
    vm = dict(zip(BACK_IN, take(len(BACK_IN))))
    dkT, dvT, delta, dP, prior_out, prior_in, g_stage, g_core, g_x, g_acc, qkv_v, wq_rows, wu_rows, gcol = take(14)
    dws = take(len(Q_HEADS))
    p, hd, row = Place(n), HD, blocks * tok
    mine, width = heads * hd, blocks * heads * hd
    share, part = width // blocks, width // 2
    per_part = part // share
    outs = {"d%d" % k: [(pl.ds(0, part), down_o.at[pl.ds(k * part, part)])] for k in range(2)}
    for k in range(2):
        outs["u%d" % k] = [
            (pl.ds(j * share, share), up_o.at[:, pl.ds((k * per_part + j) * width, width)]) for j in range(per_part)
        ]
    outs["o"] = [(pl.ds(k * share, share), out_o.at[:, pl.ds(k * part, part)]) for k in range(2)]
    plans = back_sums(n, width, share, part, mine)
    bufs = [take(len(Sum.scratch(q[1], q[2], 16, 128, n, q[0] in outs))) for q in plans]
    c = Copies(refs.pop(0))
    for name in BACK_IN:
        src = (lambda: hbm["x"].at[:, 0, :]) if name == "x" else (lambda name=name: hbm[name])
        c.local(name, src, lambda name=name: vm[name])
    c.local("wq rows", lambda: w_qkv.at[rows_at(p.s * share, share)], lambda: wq_rows)
    c.local("wu rows", lambda: w_up.at[rows_at(p.s * share, share)], lambda: wu_rows)
    sums = {}
    for (name, mode, far_z, arr, first, rows, cols), buf in zip(plans, bufs):
        src = None if arr is None else ((down_half, down_share) if name[0] == "d" else (gu, go))[arr]
        sums[name] = Sum(p, c, name, mode, far_z, src, first, rows, cols, buf, outs.get(name, []))
    qkv = [sums["q%d" % k] for k in range(len(Q_HEADS))]
    for k, own in enumerate(qkv):
        spot = lambda own=own: own.own.at[0, rows_at(p.s * mine, mine)]
        for what, mate in (("cross", p.cross_mate), ("chip", p.chip_mate), ("core", p.core_mate)):
            c.remote(("dw", k, what), lambda k=k, mate=mate: dws[k].at[rows_at(mate()[0] * mine, mine)], spot, mate)
        c.local(("dw", k, "own"), lambda k=k: dws[k].at[rows_at(p.s * mine, mine)], spot)
    for k in range(heads):
        c.remote(("prior", k), lambda k=k: prior_out.at[k], lambda k=k: prior_in.at[k], p.prior_row)
    for order in (1, 0):
        c.remote(("gh", order), lambda order=order: g_stage.at[order], lambda order=order: g_core.at[order], p.core_mate)
    c.remote(("gh", "x"), lambda: g_stage.at[1], lambda: g_x, p.chip_mate)
    c.local("rg", lambda: vm["gm"], lambda: rg_o.at[:, 0, :])
    c.local("qkv", lambda: qkv_v, lambda: qkv_o)

    def grad_h_part(owner):
        return dot(vm["wm"][...], dP[:, pl.ds(pl.multiple_of(owner * tok, tok), tok)])

    def core_grad(order):
        chip = lax.rem(p.chip + order, 2)
        g_stage[order] = grad_h_part(2 * chip + 1 - p.core).astype(BF16)
        c.start(("gh", order))

    def keep_grad(order):
        chip = lax.rem(p.chip + order, 2)
        g_acc[...] = grad_h_part(2 * chip + p.core)

    def chip_grad():
        c.wait(("gh", 1))
        g_stage[1] = (g_acc[...] + g_core[1].astype(F32)).astype(BF16)
        c.start(("gh", "x"))

    def own_grad():
        c.wait(("gh", 0))
        g_acc[...] += g_core[0].astype(F32)

    def input_grad():
        c.wait("x", "gm", ("gh", "x"))
        vm["gm"][...] += norm_back(vm["x"][...], column(gain_one), g_acc[...] + g_x[...].astype(F32))
        c.start("rg")

    def send_dw(k):
        rows = slice(Q_HEADS[k][0] * 3 * hd, (Q_HEADS[k][-1] + 1) * 3 * hd)
        dws[k][...] = dot_nt(vm["hT"][...], dP[rows, :]).astype(BF16)
        c.start(*[("dw", k, what) for what in DW])

    steps = {"gh1": lambda: core_grad(1), "gh0": lambda: core_grad(0), "ghA": lambda: keep_grad(1), "ghx": chip_grad}
    steps.update({"ghB": lambda: keep_grad(0), "ghC": own_grad, "final": input_grad})
    for name, one in sums.items():
        for phase in ("p0", "p1", "p1b", "p2", "p3", "p4", "p4b", "p5", "p6"):
            steps[name + "." + phase] = getattr(one, phase)
    for k in range(len(Q_HEADS)):
        steps["dw%d" % k] = lambda k=k: send_dw(k)
        steps["q%d.p2" % k] = lambda k=k: (c.wait(*[("dw", k, what) for what in DW]), qkv[k].p2())

    def steps_at(place, **now):
        for at, names in PLAN.get(place, {}).items():
            same = None
            for want, have in zip(at, now.values()):
                same = (have == want) if same is None else same & (have == want)

            def run():
                for name in names:
                    steps[name]()

            run() if same is None else pl.when(same)(run)

    first = BACK_IN[:8]
    c.start(*first)
    greet(p.all_mates())
    steps_at("start")
    c.start(*BACK_IN[8:], "wq rows", "wu rows")
    c.wait(*first)
    dqT = vm["oT"]
    doT, kk, vv, kT, qT, lse, start = (vm[x] for x in ("doT", "k", "v", "kT", "qT", "lse", "start"))

    def make_delta(h, carry):
        rows = pl.ds(pl.multiple_of(h * hd, hd), hd)
        delta[h] = jnp.sum(doT[rows, :].astype(F32) * vm["oT"][rows, :], axis=0, keepdims=True)
        return carry

    lax.fori_loop(0, heads, make_delta, 0)
    dqT[...] = jnp.zeros_like(dqT)
    dkT[...] = jnp.zeros_like(dkT)
    dvT[...] = jnp.zeros_like(dvT)
    steps_at("ready")

    def pair(h, i, j, causal):
        hr = pl.ds(pl.multiple_of(h * hd, hd), hd)
        qs, ks = (pl.ds(pl.multiple_of(at * tok, tok), tok) for at in (i, j))
        q_blk, do_blk = qT[hr, qs], doT[hr, qs]
        s = dot(kk[h, ks, :], q_blk)
        e = jnp.exp(s - lse[h, :, qs])
        at = lax.broadcasted_iota(jnp.int32, s.shape, 0)
        keep = at >= start[:, qs] - j * tok
        if causal:
            keep = keep & (at <= lax.broadcasted_iota(jnp.int32, s.shape, 1))
        e = jnp.where(keep, e, 0.0)
        dp = dot(vv[h, ks, :], do_blk)
        ds = (e * (dp - delta[h, :, qs])).astype(BF16)
        dvT[hr, ks] += dot_nt(do_blk, e.astype(BF16))
        dkT[hr, ks] += dot_nt(q_blk, ds)
        dqT[hr, qs] += dot(kT[hr, ks], ds)

    def prior(h, carry):
        pair(h, 0, 0, False)
        hr = pl.ds(pl.multiple_of(h * hd, hd), hd)
        prior_out[h, 0:hd, :] = dkT[hr, 0:tok].astype(BF16)
        prior_out[h, hd : 2 * hd, :] = dvT[hr, 0:tok].astype(BF16)
        for k in range(heads):
            @pl.when(h == k)
            def _():
                c.start(("prior", k))
        steps_at("prior", h=h)
        return carry

    lax.fori_loop(0, heads, prior, 0)

    def close(h):
        hr = pl.ds(pl.multiple_of(h * hd, hd), hd)
        last = pl.ds(row, tok)
        dkT[hr, last] += prior_in[h, 0:hd, :].astype(F32)
        dvT[hr, last] += prior_in[h, hd : 2 * hd, :].astype(F32)
        base = h * 3 * hd
        for k, (src, at) in enumerate(((dqT, 0), (dkT, tok), (dvT, tok))):
            val = src[hr, at:]
            val = val * (1.0 / math.sqrt(hd)) if k == 0 else val
            dP[pl.ds(pl.multiple_of(base + k * hd, hd), hd), :] = val.astype(BF16)

    def head(h, carry):
        def full(t, carry):
            i = jnp.where(t < 3, 3, jnp.where(t < 5, 2, 1))
            j = jnp.where(t < 3, t + 1, jnp.where(t < 5, t - 2, 1))
            pair(h, i, j, False)
            steps_at("full", h=h, t=t)
            return carry

        lax.fori_loop(0, 6, full, 0)

        def diagonal(i, carry):
            pair(h, i, i + 1, True)
            steps_at("diagonal", h=h, i=i)
            return carry

        lax.fori_loop(0, blocks, diagonal, 0)
        for k in range(heads):
            @pl.when(h == k)
            def _():
                if k == 0:
                    c.wait("hT", "wm")
                c.wait(("prior", k))
        close(h)
        steps_at("close", h=h)
        return carry

    lax.fori_loop(0, heads, head, 0)
    steps_at("end")

    def row_of(col):
        return jnp.broadcast_to(col, (share, 128)).T[0:1, :]

    def my_gain(gain):
        gcol[...] = column(gain)
        return gcol[pl.ds(pl.multiple_of(p.s * share, share), share), :]

    c.wait("wq rows", "wu rows")
    total = jnp.zeros((share, 1), F32)
    for k in range(2):
        for j in range(per_part):
            cols = slice((k * per_part + j) * width, (k * per_part + j + 1) * width)
            prod = sums["u%d" % k].full[j * share : (j + 1) * share, :] * wu_rows[:, cols].astype(F32)
            total = total + jnp.sum(prod, axis=1, keepdims=True)
    gain_two_o[...] = row_of(total / my_gain(gain_two))
    total = jnp.zeros((share, 1), F32)
    for k in range(3):
        for s in range(blocks):
            cells = []
            for own, hs in zip(qkv, Q_HEADS):
                for h in range(len(hs)):
                    at = (h * 3 + k) * hd
                    cells.append(own.res[s * share : (s + 1) * share, at : at + hd])
            cells = jnp.concatenate(cells, axis=1).astype(F32)
            cols = slice(k * width + s * mine, k * width + (s + 1) * mine)
            qkv_v[:, cols] = cells
            total = total + jnp.sum(cells * wq_rows[:, cols].astype(F32), axis=1, keepdims=True)
    gain_one_o[...] = row_of(total / my_gain(gain_one))
    c.start("qkv")
    for one in sums.values():
        one.p7()
    c.wait("qkv", "rg")


def back_pass(n, tok, blocks, ins, down_half, down_share, gu, go, w_qkv, w_up, gain_one, gain_two):
    heads = ins[1].shape[0]
    row = blocks * tok
    width = ins[8].shape[0]
    mine = heads * HD
    parts, share, part = w_up.shape[1] // width, width // blocks, width // 2
    v = lambda *s, t=BF16: pltpu.VMEM(s, t)
    o = lambda *s: jax.ShapeDtypeStruct(s, F32)
    scratch = [v(width - 1, tok, t=F32) if name == "x" else pltpu.VMEM(a.shape, a.dtype) for name, a in zip(BACK_IN, ins)]
    scratch += [
        v(mine, row + tok, t=F32), v(mine, row + tok, t=F32), v(heads, 1, row, t=F32), v(3 * mine, row),
        v(heads, 2 * HD, tok), v(heads, 2 * HD, tok),
        v(2, width, tok), v(2, width, tok), v(width, tok), v(width, tok, t=F32), v(share, 3 * width, t=F32),
        v(share, 3 * width), v(share, w_up.shape[1]), v(width, 1, t=F32),
    ]
    scratch += [v(width, mine * len(hs)) for hs in Q_HEADS]
    copies = len(ins) + 5 * heads + 8
    for name, mode, far_z, _, _, rows, cols in back_sums(n, width, share, part, mine):
        scratch += Sum.scratch(mode, far_z, rows, cols, n, name[0] != "q")
        copies += 17 + n // 8
    scratch.append(pltpu.SemaphoreType.DMA((2, copies)))
    hbm = pl.BlockSpec(memory_space=pl.ANY)
    vmem = pl.BlockSpec(memory_space=pltpu.VMEM)
    return pl.pallas_call(
        functools.partial(back_kernel, n, tok, blocks, heads, parts),
        out_shape=[
            o(width, width), o(share, parts * width), o(share, width), o(share, 3 * width),
            o(1, share), o(1, share), o(width - 1, 1, tok),
        ],
        in_specs=[hbm] * (len(ins) + 6) + [vmem, vmem],
        out_specs=[hbm] * 4 + [vmem, vmem, hbm],
        scratch_shapes=scratch,
        compiler_params=pltpu.CompilerParams(collective_id=1, has_side_effects=True, vmem_limit_bytes=VMEM_LIMIT),
    )(*ins, down_half, down_share, gu, go, w_qkv, w_up, gain_one, gain_two)


def per_device(residual, documents, gain_one, gain_two, w_qkv, w_out, w_up, w_down, cotangent):
    blocks = lax.axis_size("seq")
    n = lax.axis_size("batch")
    tok = residual.shape[1]
    x = jnp.transpose(residual, (2, 0, 1))
    cot = jnp.transpose(cotangent, (2, 0, 1))
    attT, hT, kT, qT, oT, lse, start, k, v, w_mine = fore_pass(n, tok, blocks, x, gain_one, documents, w_qkv)
    new, grad_middle, doT, grad_up, grad_out, down_half, down_share = mid_pass(
        n, blocks, x, cot, attT, gain_two, w_out, w_up, w_down
    )
    sum_down, sum_up, sum_out, sum_qkv, one, two, grad_x = back_pass(
        n, tok, blocks, (doT, k, v, kT, qT, oT, lse, start, hT, w_mine, x, grad_middle),
        down_half, down_share, grad_up, grad_out, w_qkv, w_up, gain_one, gain_two,
    )
    new, grad_x = jnp.transpose(new, (1, 2, 0)), jnp.transpose(grad_x, (1, 2, 0))
    return (new, grad_x, one[0], two[0], sum_qkv, sum_out, sum_up, sum_down)


def solution(mesh):
    placed = (
        P("batch", "seq", None),
        P("batch", "seq"),
        P(),
        P(),
        P(),
        P(),
        P(),
        P(),
        P("batch", "seq", None),
    )
    return jax.shard_map(
        per_device,
        mesh=mesh,
        in_specs=placed,
        out_specs=(
            P("batch", "seq", None),
            P("batch", "seq", None),
            P("seq"),
            P("seq"),
            P("seq", None),
            P("seq", None),
            P("seq", None),
            P("seq", None),
        ),
        check_vma=False,
    )
```

time: 237 us -> 200 us (0.84)
  Pallas kernels: 219 us -> 188 us
  other arithmetic: 8.39 us -> 0 us
    pallas_call x1, Pallas kernels: 132 us -> 105 us  [back_pass(): pl.pallas_call(functools.partial(back_kernel, n, tok, blocks, heads, part...]
    convert_element_type x3 -> x0, other arithmetic: 6.42 us -> none  [the longest x1 3.03 us: per_device(): sum_up.astype(F32)]
    unnamed x13 -> x24, local copies, waits for them, and re-layouts: 5.77 us -> 10.8 us
    pallas_call x1, Pallas kernels: 50.3 us -> 46.9 us  [fore_pass(): pl.pallas_call(functools.partial(fore_kernel, n, tok, blocks, heads), out...]
where the time goes in v1:
time: 200 us
  Pallas kernels  188 us (94%)
  local copies, waits for them, and re-layouts  10.8 us (5%)
    pallas_call x1, Pallas kernels, back_pass(): pl.pallas_call(functools.partial(back_kernel, n, tok, blocks, heads, part...  105 us
    pallas_call x1, Pallas kernels, fore_pass(): pl.pallas_call(functools.partial(fore_kernel, n, tok, blocks, heads), out...  46.9 us
    pallas_call x1, Pallas kernels, mid_pass(): pl.pallas_call(functools.partial(mid_kernel, n, blocks), out_shape=[o(wid...  36.1 us
    unnamed x24, local copies, waits for them, and re-layouts  10.8 us

profile of v1, /device:TPU:0, one launch (start us, length us, event | category | flops | bytes accessed | tf_op | source)
XLA Modules:
  0.0 199.5 jit_solution(2428948216850668044)
XLA Ops:
  0.6 46.9 %shard_map.152 = (bf16[768,512]{1,0:T(8,128)(2,1)}, bf16[768,2048]{1,0:T(8,128)(2,1)}, bf16[192,2560]{1,0:T(8,128)(2,1)}, bf16[192,2048]{1,0:T(8,128)(2,1)}, f32...) custom-call(f32[767,1,512]{2,1,0:T(1,128)} %bitcast.6, ...), custom_call_target="tpu_custom_call" | custom-call | tf_op jit(solution)/shard_map/pallas_call | solution.py:594
  47.5 36.1 %shard_map.153 = (f32[767,1,512]{2,1,0:T(1,128)}, f32[767,512]{1,0:T(8,128)}, bf16[192,2048]{1,0:T(8,128)(2,1)}, bf16[4,768,768]{2,1,0:T(8,128)(2,1)}, bf16[4,38...) custom-call(f32[767,1,512]{2,1,0:T(1,128)} %bitcast.7, f32[767,1,512]{2,1,0:T(1,128)} %bitcast.9, ...), custom_call_target="tpu_custom_call" | custom-call | tf_op jit(solution)/shard_map/pallas_call | solution.py:761
  83.6 0.0 copy-start.3
  83.7 105.0 %shard_map.154 = (f32[768,768]{1,0:T(8,128)}, f32[192,3072]{1,0:T(8,128)}, f32[192,768]{1,0:T(8,128)}, f32[192,2304]{1,0:T(8,128)}, f32[1,192]{1,0:T(1,128)}, /*index=5*/f32[1,192]{1,0:T(1,128)}, f32[767,1,512]{2,1,0:T(1,128)}) custom-call(bf16[192,2048]{1,0:T(8,128)(2,1)} %get-tuple-element.34.refs_0_, bf16[3,2560,64]{2,1,0:T(8,128)(2,1)} %get-tuple-element.35.refs_1_, ...), custom_call_target="tpu_custom_call" | custom-call | tf_op jit(solution)/shard_map/pallas_call | solution.py:1067
  188.7 0.0 copy-start.4
  188.7 0.0 copy-done.3
  188.7 1.1 copy.25
  189.8 0.8 copy-done.4
  190.6 0.0 copy-start.7
  190.7 0.0 copy-start.6
  190.7 0.0 copy-start.2
  190.7 1.1 copy.26
  191.8 0.0 copy-done.7
  191.8 0.6 copy.27
  192.4 0.0 copy-done.6
  192.4 0.6 copy.28
  192.9 0.0 copy-done.2
  192.9 0.0 copy-start.5
  192.9 0.0 copy-start.1
  192.9 1.2 copy.29
  194.1 0.2 copy-done.5
  194.4 0.8 copy.30
  195.2 0.4 copy-done.1
  195.6 0.0 copy-start
  195.6 1.4 copy.31
  197.0 1.1 copy-done
  198.1 1.4 copy.32
Async XLA Ops:
  83.6 105.0 %copy-start.3 = (f32[767,1,512]{2,1,0:T(1,128)S(1)}, f32[767,1,512]{2,1,0:T(1,128)}, u32[]{:S(2)}) copy-start(f32[767,1,512]{2,1,0:T(1,128)} %get-tuple-element.33) | copy-start | bytes 4712452
  188.7 2.0 copy-start.4
  190.6 1.1 copy-start.7
  190.7 1.7 copy-start.6
  190.7 2.3 %copy-start.2 = (f32[192,2304]{1,0:T(8,128)S(1)}, f32[192,2304]{1,0:T(8,128)}, u32[]{:S(2)}) copy-start(f32[192,2304]{1,0:T(8,128)} %get-tuple-element.68) | copy-start | bytes 5308420
  192.9 1.4 copy-start.5
  192.9 2.7 %copy-start.1 = (f32[192,3072]{1,0:T(8,128)S(1)}, f32[192,3072]{1,0:T(8,128)}, u32[]{:S(2)}) copy-start(f32[192,3072]{1,0:T(8,128)} %get-tuple-element.70) | copy-start | bytes 7077892
  195.6 2.5 %copy-start = (f32[768,768]{1,0:T(8,128)S(1)}, f32[768,768]{1,0:T(8,128)}, u32[]{:S(2)}) copy-start(f32[768,768]{1,0:T(8,128)} %get-tuple-element.71) | copy-start | bytes 7077892

commit v2 on v1

--- a/solution.py
+++ b/solution.py
@@ -177,43 +177,47 @@
     lax.fori_loop(0, rows // step, one, 0)
 
 
+PAIRS, QUARTERS, PAIRS_Z = range(3)
+
+
 class Sum:
-    def __init__(self, place, copies, name, mode, far_z, src, first, rows, cols, bufs, out):
-        self.p, self.c, self.name, self.mode, self.far_z = place, copies, name, mode, far_z
+    def __init__(self, place, copies, name, mode, way, src, first, rows, cols, bufs, out):
+        self.p, self.c, self.name, self.mode, self.way = place, copies, name, mode, way
+        bits = [(place.y, place.y_mate), (lax.rem(place.z, 2), lambda: place.z_pair(1))]
+        (self.one, self.one_mate), (self.two, self.two_mate) = bits[::-1] if way == PAIRS_Z else bits
         self.src, self.first, self.rows, self.cols, self.out = src, first, rows, cols, out
         bufs = list(bufs)
-        self.full = bufs.pop(0) if out else None
         self.own, self.ry, self.rz, self.res, self.rf = bufs[:5]
         self.rc = bufs[5] if mode in "xy" else None
-        self.rx = bufs[-1] if mode != "share" else None
+        self.rx = bufs[-1] if mode not in ("share", "ready") else None
         self.mine = (lambda: self.own.at[self.p.chip]) if mode in "xy" else (lambda: self.own.at[0])
         self.define()
 
     @staticmethod
-    def scratch(mode, far_z, rows, cols, n, full):
+    def scratch(mode, way, rows, cols, n):
         def v(*s):
             return pltpu.VMEM(s, BF16)
 
-        half, spot = rows // 2, rows // (8 if far_z else 4)
+        half, spot = rows // 2, rows // (8 if way == QUARTERS else 4)
         out = [v(2 if mode in "xy" else 1, rows, cols), v(2 if mode == "y" else 1, half, cols)]
-        out += [v(3 if far_z else 2, spot, cols), v(rows, cols), v(n // 8 if n > 8 else 1, spot if n > 8 else 16, cols)]
+        out += [v(3 if way == QUARTERS else 2, spot, cols), v(rows, cols), v(n // 8 if n > 8 else 1, spot if n > 8 else 16, cols)]
         if mode in "xy":
             out.append(v(2, rows, cols))
-        if mode != "share":
+        if mode not in ("share", "ready"):
             out.append(v(rows if mode == "x" else half, cols))
-        return [pltpu.VMEM((rows, cols), F32)] + out if full else out
+        return out
 
     def id(self, what):
         return (self.name, what)
 
-    def at_half(self, y):
-        return rows_at(y * (self.rows // 2), self.rows // 2)
+    def at_half(self, one):
+        return rows_at(one * (self.rows // 2), self.rows // 2)
 
     def at_spot(self):
         p, half = self.p, self.rows // 2
-        if self.far_z:
+        if self.way == QUARTERS:
             return rows_at(p.y * half + p.z * (half // 4), half // 4)
-        return rows_at(p.y * half + lax.rem(p.z, 2) * (half // 2), half // 2)
+        return rows_at(self.one * half + self.two * (half // 2), half // 2)
 
     def define(self):
         p, c, half, far = self.p, self.c, self.rows // 2, self.p.n // 8
@@ -236,17 +240,17 @@
         if self.mode == "x":
             c.remote(self.id("x"), other, lambda: self.rx, p.chip_mate)
         if self.mode == "y":
-            c.remote(self.id("y1"), lambda: other().at[self.at_half(1 - p.y)], lambda: self.ry.at[1], p.y_mate)
-            c.remote(self.id("x"), lambda: other().at[self.at_half(p.y)], lambda: self.rx, p.chip_mate)
-        if self.mode == "share" and self.src is not None:
-            c.local(self.id("own"), lambda: self.src, lambda: self.own.at[0])
+            c.remote(self.id("y1"), lambda: other().at[self.at_half(1 - self.one)], lambda: self.ry.at[1], self.one_mate)
+            c.remote(self.id("x"), lambda: other().at[self.at_half(self.one)], lambda: self.rx, p.chip_mate)
+        if self.mode == "ready":
+            c.local(self.id("own"), lambda: self.src, lambda: self.own.at[0, self.at_half(self.one)])
         if self.mode == "half":
             c.remote(self.id("x"), lambda: self.src.at[1 - p.chip], lambda: self.rx, p.chip_mate)
-            c.local(self.id("own"), lambda: self.src.at[p.chip], lambda: self.own.at[0, self.at_half(p.y)])
-        else:
-            c.remote(self.id("y"), lambda: self.mine().at[self.at_half(1 - p.y)], lambda: self.ry.at[0], p.y_mate)
+            c.local(self.id("own"), lambda: self.src.at[p.chip], lambda: self.own.at[0, self.at_half(self.one)])
+        elif self.mode != "ready":
+            c.remote(self.id("y"), lambda: self.mine().at[self.at_half(1 - self.one)], lambda: self.ry.at[0], self.one_mate)
         spot = lambda: self.res.at[self.at_spot()]
-        if self.far_z:
+        if self.way == QUARTERS:
             for d in (2, 1, 3):
                 c.remote(
                     self.id(("z", d)),
@@ -256,16 +260,16 @@
                 )
                 c.remote(self.id(("back z", d)), spot, spot, lambda d=d: p.z_mate(d))
         else:
-            away = lambda: rows_at(p.y * half + (1 - lax.rem(p.z, 2)) * (half // 2), half // 2)
-            c.remote(self.id("z1"), lambda: self.mine().at[away()], lambda: self.rz.at[0], lambda: p.z_pair(1))
+            away = lambda: rows_at(self.one * half + (1 - self.two) * (half // 2), half // 2)
+            c.remote(self.id("z1"), lambda: self.mine().at[away()], lambda: self.rz.at[0], self.two_mate)
             c.remote(self.id("z2"), lambda: self.mine().at[self.at_spot()], lambda: self.rz.at[1], lambda: p.z_pair(2))
-            c.remote(self.id("back z1"), spot, spot, lambda: p.z_pair(1))
+            c.remote(self.id("back z1"), spot, spot, self.two_mate)
         for d in range(1, far):
             c.remote(self.id(("far", d)), lambda: self.rf.at[p.far], lambda: self.rf.at[p.far], lambda d=d: p.far_mate(d))
-        my_half = lambda: self.res.at[self.at_half(p.y)]
-        c.remote(self.id("back y"), my_half, my_half, p.y_mate)
+        my_half = lambda: self.res.at[self.at_half(self.one)]
+        c.remote(self.id("back y"), my_half, my_half, self.one_mate)
         for k, (src, dst) in enumerate(self.out):
-            c.local(self.id(("out", k)), lambda src=src: self.full.at[src], lambda dst=dst: dst)
+            c.local(self.id(("out", k)), lambda src=src: self.res.at[src], lambda dst=dst: dst)
 
     def add(self, dst, at, rows, *others):
         def body(first, step):
@@ -280,7 +284,7 @@
     def p0(self):
         if self.mode == "half":
             self.c.start(self.id("x"), self.id("own"))
-        if self.mode == "share":
+        if self.mode == "ready":
             self.c.start(self.id("own"))
         if self.mode in "xy":
             for order in (1, 0):
@@ -299,33 +303,31 @@
             self.c.start(self.id("y"))
 
     def p2(self):
-        p, half = self.p, self.rows // 2
+        half = self.rows // 2
         if self.mode == "y":
             self.c.wait(self.id("y1"))
-            self.add(self.own.at[1 - p.chip], p.y * half, half, (self.ry.at[1], 0))
+            self.add(self.own.at[1 - self.p.chip], self.one * half, half, (self.ry.at[1], 0))
             self.c.start(self.id("x"))
             return
         if self.mode == "x":
             self.c.wait(self.id("x"))
-            self.add(self.mine(), (1 - p.y) * half, half, (self.rx, (1 - p.y) * half))
-        if self.mode == "share" and self.src is not None:
-            self.c.wait(self.id("own"))
+            self.add(self.mine(), (1 - self.one) * half, half, (self.rx, (1 - self.one) * half))
         self.c.start(self.id("y"))
 
     def p3(self):
-        p, half, more = self.p, self.rows // 2, []
-        if self.mode != "half":
+        half, more = self.rows // 2, []
+        if self.mode not in ("half", "ready"):
             self.c.wait(self.id("y"))
             more.append((self.ry.at[0], 0))
         if self.mode == "x":
-            more.append((self.rx, p.y * half))
+            more.append((self.rx, self.one * half))
         if self.mode in ("y", "half"):
             self.c.wait(self.id("x"))
             more.append((self.rx, 0))
-        if self.mode == "half":
+        if self.mode in ("half", "ready"):
             self.c.wait(self.id("own"))
-        self.add(self.mine(), p.y * half, half, *more)
-        self.c.start(*([self.id(("z", d)) for d in (2, 1, 3)] if self.far_z else [self.id("z1")]))
+        self.add(self.mine(), self.one * half, half, *more)
+        self.c.start(*([self.id(("z", d)) for d in (2, 1, 3)] if self.way == QUARTERS else [self.id("z1")]))
 
     def total(self, *others):
         p = self.p
@@ -358,7 +360,7 @@
             blockwise(rows, more)
 
     def p4(self):
-        if self.far_z:
+        if self.way == QUARTERS:
             self.c.wait(*[self.id(("z", d)) for d in (1, 2, 3)])
             self.total(*[self.rz.at[d] for d in range(3)])
             self.c.start(*[self.id(("back z", d)) for d in (2, 1, 3)])
@@ -369,29 +371,27 @@
         self.c.start(self.id("z2"))
 
     def p4b(self):
-        if not self.far_z:
+        if not self.way == QUARTERS:
             self.c.wait(self.id("z2"))
             self.total(self.rz.at[1])
             self.c.start(self.id("back z1"))
 
     def p5(self):
-        self.c.wait(*([self.id(("back z", d)) for d in (1, 2, 3)] if self.far_z else [self.id("back z1")]))
+        self.c.wait(*([self.id(("back z", d)) for d in (1, 2, 3)] if self.way == QUARTERS else [self.id("back z1")]))
         self.c.start(self.id("back y"))
 
     def p6(self):
         self.c.wait(self.id("back y"))
-        if not self.out:
-            return
-
-        def body(first, step):
-            here = rows_at(first, step)
-            self.full[here, :] = self.res[here, :].astype(F32)
-
-        blockwise(self.rows, body)
         self.c.start(*[self.id(("out", k)) for k in range(len(self.out))])
 
     def p7(self):
         self.c.wait(*[self.id(("out", k)) for k in range(len(self.out))])
+
+    def phase(self, k):
+        (self.p0, self.p1, self.p1b, self.p2, self.p3, self.p4, self.p4b, self.p5, self.p6)[k]()
+
+
+PRIOR_KV = (("prior k", 0), ("prior k", 1), ("prior v", 0), ("prior v", 1))
 
 
 def fore_kernel(n, tok, blocks, heads, *refs):
@@ -406,7 +406,6 @@
     mates = {"core": p.core_mate, "chip": p.chip_mate, "cross": p.cross_mate}
     block = lambda at: pl.ds(pl.multiple_of(at * tok, tok), tok)
     here = lambda: block(p.s)
-    c.local("x", lambda: x.at[:, 0, :], lambda: xs)
     c.local("w", lambda: w, lambda: ws)
     c.local("docs", lambda: docs, lambda: docs_all.at[:, here()])
     for name, mate in mates.items():
@@ -416,13 +415,15 @@
     c.remote("h core", lambda: hT.at[:, here()], lambda: hT.at[:, here()], p.core_mate)
     half = tok // 2
     for k in range(2):
+        c.local(("x", k), lambda k=k: x.at[:, 0, pl.ds(k * half, half)], lambda k=k: xs.at[:, pl.ds(k * half, half)])
         piece = lambda s, k=k: hT.at[:, pl.ds(pl.multiple_of(s * tok + k * half, half), half)]
         c.remote(("h chip", k), lambda piece=piece: piece(p.s), lambda piece=piece: piece(p.s), p.chip_mate)
         other = lambda piece=piece: piece(p.chip_mate()[0])
         c.remote(("h on", k), other, other, p.core_mate)
-    end = pl.ds(row, tok)
-    c.remote("prior k", lambda: kT.at[:, end], lambda: kT.at[:, 0:tok], p.next_row)
-    c.remote("prior v", lambda: vT.at[:, end], lambda: vT.at[:, 0:tok], p.next_row)
+    for k in range(2):
+        end, to = pl.ds(row + k * half, half), pl.ds(k * half, half)
+        c.remote(("prior k", k), lambda end=end: kT.at[:, end], lambda to=to: kT.at[:, to], p.next_row)
+        c.remote(("prior v", k), lambda end=end: vT.at[:, end], lambda to=to: vT.at[:, to], p.next_row)
     for h in range(heads):
         spot = lambda h=h: attT_o.at[pl.ds(pl.multiple_of(p.s * mine + h * HD, HD), HD)]
         for name, mate in mates.items():
@@ -434,14 +435,17 @@
     for name, (src, dst) in outs.items():
         c.local(("out", name), lambda src=src: src, lambda dst=dst: dst)
 
-    c.start("x", "docs", "w")
+    c.start(("x", 0), ("x", 1), "docs", "w")
     greet([p.core_mate(), p.chip_mate(), p.cross_mate(), p.next_row(), p.prior_row()])
     c.start(*[("docs", name) for name in mates])
-    c.wait("x")
-    full_vec = expand(xs[...])
-    hT[:, here()] = (column(gain) * full_vec * root(full_vec)).astype(BF16)
-    c.start(("h chip", 0), "h core")
-    c.start(("h chip", 1))
+    gain_col = column(gain)
+    for k in range(2):
+        c.wait(("x", k))
+        full_vec = expand(xs[:, k * half : (k + 1) * half])
+        mine_now = pl.ds(pl.multiple_of(p.s * tok + k * half, half), half)
+        hT[:, mine_now] = (gain_col * full_vec * root(full_vec)).astype(BF16)
+        c.start(("h chip", k))
+    c.start("h core")
 
     c.wait("w")
     for s in range(blocks):
@@ -467,28 +471,28 @@
     l_ref[...] = jnp.zeros(l_ref.shape, F32)
     acc[...] = jnp.zeros(acc.shape, F32)
 
-    def natural(keys_at):
-        keys = pl.ds(pl.multiple_of(keys_at, tok), tok)
+    def natural(keys_at, count):
+        keys = pl.ds(pl.multiple_of(keys_at, 128), count)
         for h in range(heads):
             kk[h, keys, :] = kT[h * HD : (h + 1) * HD, keys].T
             vv[h, keys, :] = vT[h * HD : (h + 1) * HD, keys].T
 
-    def project(at):
-        packed = dot_tn(wm[...], hT[:, block(at)]).astype(BF16)
-        keys = pl.ds(pl.multiple_of((at + 1) * tok, tok), tok)
+    def project(at, count):
+        own, keys = pl.ds(pl.multiple_of(at, 128), count), pl.ds(pl.multiple_of(at + tok, 128), count)
+        packed = dot_tn(wm[...], hT[:, own]).astype(BF16)
         for h in range(heads):
             to, base = slice(h * HD, (h + 1) * HD), h * 3 * HD
-            qT[to, block(at)] = packed[base : base + HD] * jnp.bfloat16(1.0 / math.sqrt(HD))
+            qT[to, own] = packed[base : base + HD] * jnp.bfloat16(1.0 / math.sqrt(HD))
             kT[to, keys] = packed[base + HD : base + 2 * HD]
             vT[to, keys] = packed[base + 2 * HD : base + 3 * HD]
-        natural((at + 1) * tok)
-
-    def pair(h, i, j, size, causal):
+        natural(at + tok, count)
+
+    def pair(h, q0, qw, k0, kw, causal):
         hr = pl.ds(pl.multiple_of(h * HD, HD), HD)
-        qs, ks = (pl.ds(pl.multiple_of(at * tok, tok), size) for at in (i, j))
+        qs, ks = pl.ds(pl.multiple_of(q0, 128), qw), pl.ds(pl.multiple_of(k0 + tok, 128), kw)
         s = dot(kk[h, ks, :], qT[hr, qs])
         at = lax.broadcasted_iota(jnp.int32, s.shape, 0)
-        keep = at >= start[:, qs] - j * tok
+        keep = at >= start[:, qs] - (k0 + tok)
         if causal:
             keep = keep & (at <= lax.broadcasted_iota(jnp.int32, s.shape, 1))
         s = jnp.where(keep, s, NEG)
@@ -513,38 +517,52 @@
             def _():
                 c.start(("att", h, name))
 
-    near, far = 2 * p.chip, 2 * (1 - p.chip)
+    pair_rows = 2 * tok
+    near, far = pair_rows * p.chip, pair_rows * (1 - p.chip)
     c.wait_recv("h core")
-
-    def project_near(t, carry):
-        project(near + t)
-        return carry
-
-    lax.fori_loop(0, 2, project_near, 0)
+    lax.fori_loop(0, 2, lambda t, carry: (project(near + t * tok, tok), carry)[1], 0)
+
+    def send_prior(k):
+        c.start(("prior k", k), ("prior v", k))
 
     @pl.when(p.chip == 1)
     def _():
-        c.start("prior k", "prior v")
-
-    def first(h, carry):
-        pair(h, near, near + 1, 2 * tok, True)
-        return carry
-
-    lax.fori_loop(0, heads, first, 0)
-    for k in range(2):
+        send_prior(0)
+        send_prior(1)
+
+    lax.fori_loop(0, heads, lambda h, carry: (pair(h, near, pair_rows, near, pair_rows, True), carry)[1], 0)
+
+    def far_half(k):
         c.wait_recv(("h chip", k))
         c.start(("h on", k))
-    project(p.chip_mate()[0])
-    c.wait_recv(("h on", 0), ("h on", 1))
-    project(p.cross_mate()[0])
-
-    @pl.when(p.chip == 0)
-    def _():
-        c.start("prior k", "prior v")
+        project(p.chip_mate()[0] * tok + k * half, half)
+        c.wait_recv(("h on", k))
+        project(p.cross_mate()[0] * tok + k * half, half)
+
+        def queries(h, carry):
+            for i in range(2):
+                pair(h, pair_rows + i * tok + k * half, half, 0, pair_rows, False)
+            return carry
+
+        def keys(h, carry):
+            for i in range(2):
+                pair(h, pair_rows, pair_rows, i * tok + k * half, half, False)
+            return carry
+
+        @pl.when(p.chip == 0)
+        def _():
+            send_prior(k)
+            lax.fori_loop(0, heads, queries, 0)
+
+        @pl.when(p.chip == 1)
+        def _():
+            lax.fori_loop(0, heads, keys, 0)
+
+    far_half(0)
+    far_half(1)
 
     def second(h, carry):
-        pair(h, far, far + 1, 2 * tok, True)
-        pair(h, 2, 1, 2 * tok, False)
+        pair(h, far, pair_rows, far, pair_rows, True)
         lax.fori_loop(1, blocks, lambda i, carry: (finish(h, i), carry)[1], 0)
         for k in range(heads):
             @pl.when(h == k)
@@ -558,11 +576,11 @@
     at = lax.broadcasted_iota(jnp.int32, (1, tok), 1)
     run = jnp.max(jnp.where(prior_docs[...] != from_doc, at + 1, 0), axis=1, keepdims=True)
     start[:, 0:tok] = jnp.where(start[:, 0:tok] == tok, run, start[:, 0:tok])
-    c.wait_recv("prior k", "prior v")
-    natural(0)
+    c.wait_recv(*PRIOR_KV)
+    natural(0, tok)
 
     def third(h, carry):
-        pair(h, 0, 0, tok, False)
+        pair(h, 0, tok, -tok, tok, False)
         finish(h, 0)
         for k in range(heads):
             @pl.when(h == k)
@@ -572,7 +590,7 @@
 
     lax.fori_loop(0, heads, third, 0)
     c.start(*[("out", name) for name in outs])
-    c.wait_send("h core", ("h chip", 0), ("h chip", 1), ("h on", 0), ("h on", 1), "prior docs", "prior k", "prior v")
+    c.wait_send("h core", ("h chip", 0), ("h chip", 1), ("h on", 0), ("h on", 1), "prior docs", *PRIOR_KV)
     for h in range(heads):
         c.wait(*[("att", h, name) for name in list(mates) + ["own"]])
     c.wait(*[("out", name) for name in outs])
@@ -589,7 +607,7 @@
         v(1, row, t=jnp.int32), v(1, tok, t=jnp.int32), v(1, row, t=jnp.int32),
         v(mine, row + tok), v(mine, row + tok), v(mine, row), v(heads, row + tok, HD), v(heads, row + tok, HD),
         v(mine, row, t=F32), v(heads, 1, row, t=F32), v(heads, 1, row, t=F32), v(heads, 1, row, t=F32), v(mine, row),
-        pltpu.SemaphoreType.DMA((2, 24 + 4 * heads)),
+        pltpu.SemaphoreType.DMA((2, 27 + 4 * heads)),
     ]
     return pl.pallas_call(
         functools.partial(fore_kernel, n, tok, blocks, heads),
@@ -615,7 +633,7 @@
 
 def mid_kernel(n, blocks, *refs):
     x, cot, attT, gain, w_out, w_up, w_down = refs[:7]
-    new_o, gm_o, doT_o, gu_o, go_o, half_o, share_o = refs[7:14]
+    new_o, gm_o, doT_o, gu_o, go_o, half_o, ready_o = refs[7:14]
     xs, cs, at, wo, wu, wd, mid, h2, g2, g1, geluT, gupT, b2, gh, dw, rc, ry, rx, ga, gu, go, sems = refs[14:]
     tok, width = xs.shape[1], xs.shape[0] + 1
     parts = wu.shape[1] // width
@@ -640,7 +658,9 @@
         c.local(("half", t), lambda t=t: dw.at[2 * t + 1, low(p.y)], dst)
     high = pl.ds(part, part)
     c.remote("chip", lambda: dw.at[1, high], lambda: rx, p.chip_mate)
-    c.local("share", lambda: dw.at[3, high], lambda: share_o)
+    later = lambda y: rows_at(part + y * fourth, fourth)
+    c.remote(("y", 2), lambda: dw.at[3, later(1 - p.y)], lambda: ry.at[2], p.y_mate)
+    c.local("ready", lambda: dw.at[3, later(p.y)], lambda: ready_o)
     there = lambda: doT_o.at[:, pl.ds(pl.multiple_of(p.s * tok, tok), tok)]
     for name, mate in mates.items():
         c.remote(("ga", name), lambda mate=mate: ga.at[rows_at(mate()[0] * share, share)], there, mate)
@@ -728,21 +748,25 @@
             gu[s, rows_at(k * share, share), :] = grad[s * share : (s + 1) * share]
         return carry
 
-    lax.fori_loop(0, parts, up_grad, 0)
+    lax.fori_loop(0, parts // 2, up_grad, 0)
+    c.wait("chip")
+    add(3, part, rx, part)
+    c.start(("y", 2))
+    lax.fori_loop(parts // 2, parts, up_grad, 0)
     c.start(*[("gu", k) for k in range(parts)])
     out_grad = dot_nt(at[...], g1[...]).astype(BF16)
     for s in range(blocks):
         for k in range(2):
             go[s, k * share : (k + 1) * share, :] = out_grad[s * share : (s + 1) * share, k * part : (k + 1) * part]
     c.start("go")
-    c.wait("chip")
-    add(3, part, rx, part)
-    c.start("share")
     y_sum(0)
     y_sum(1)
+    c.wait(("y", 2))
+    add(3, part + p.y * fourth, ry.at[2], fourth)
+    c.start("ready")
     c.wait_send("core 0", "core 1")
     c.wait(*[("ga", name) for name in list(mates) + ["own"]])
-    c.wait("gm", "new out", "go", "share", ("half", 0), ("half", 1), *[("gu", k) for k in range(parts)])
+    c.wait("gm", "new out", "go", "ready", ("half", 0), ("half", 1), *[("gu", k) for k in range(parts)])
 
 
 def mid_pass(n, blocks, x, cot, attT, gain, w_out, w_up, w_down):
@@ -754,7 +778,7 @@
     scratch = [
         v(width - 1, tok, t=F32), v(width - 1, tok, t=F32), v(width, tok), v(width, width), v(*w_up.shape), v(*w_down.shape),
         v(width - 1, tok, t=F32), v(width, tok), v(width, tok), v(width, tok), v(width, tok), v(w_up.shape[1], tok),
-        v(width, tok, t=F32), v(width, tok, t=F32), v(4, width, width), v(2, width, width), v(2, width // 4, width), v(width // 2, width),
+        v(width, tok, t=F32), v(width, tok, t=F32), v(4, width, width), v(2, width, width), v(3, width // 4, width), v(width // 2, width),
         v(width, tok), v(blocks, parts * share, width), v(blocks, 2 * share, width // 2),
         pltpu.SemaphoreType.DMA((2, 32)),
     ]
@@ -762,7 +786,7 @@
         functools.partial(mid_kernel, n, blocks),
         out_shape=[
             o(width - 1, 1, tok, t=F32), o(width - 1, tok, t=F32), o(share, blocks * tok), o(blocks, parts * share, width),
-            o(blocks, 2 * share, width // 2), o(2, width // 4, width), o(width // 2, width),
+            o(blocks, 2 * share, width // 2), o(2, width // 4, width), o(width // 4, width),
         ],
         in_specs=[hbm, hbm, hbm, pl.BlockSpec(memory_space=pltpu.VMEM), hbm, hbm, hbm],
         out_specs=[hbm] * 7,
@@ -773,96 +797,107 @@
 
 BACK_IN = ("doT", "k", "v", "kT", "qT", "oT", "lse", "start", "hT", "wm", "x", "gm")
 DW = ("cross", "chip", "core", "own")
+D0, D1, U0, U1, O, Q0, Q1, GRAD_H, SEND = range(9)
 Q_HEADS = ((0, 1), (2,))
 U_MODES = ("x", "x")
 O_MODE = "y"
-FAR_Z = {"d": True, "u": False, "o": False, "q": False}
+WAYS = (PAIRS, PAIRS, PAIRS, PAIRS, PAIRS, PAIRS_Z, PAIRS)
+START, READY, PRIOR, FULL, DIAGONAL, CLOSE, END = range(7)
 PLAN = {
-    "start": {
-        (): ["d0.p0", "u1.p0", "u0.p0", "d1.p0", "o.p0"],
+    START: {
+        (): [(D0, 0), (U1, 0), (U0, 0), (D1, 0), (O, 0)],
     },
-    "ready": {
-        (): ["u1.p1", "d1.p2"],
+    READY: {
+        (): [(U1, 1), (D1, 4)],
     },
-    "prior": {
-        (0,): ["u1.p1b", "u0.p1"],
-        (1,): ["u0.p1b", "o.p1", "d0.p3", "o.p1b"],
+    PRIOR: {
+        (0,): [(U1, 2)],
+        (1,): [(U0, 1), (U0, 2)],
+        (2,): [(D0, 4), (D1, 5), (O, 1), (O, 2)],
     },
-    "full": {
-        (0, 1): ["d1.p3"],
-        (1, 2): ["d0.p4"],
-        (2, 2): ["o.p3"],
-        (2, 5): ["d0.p5"],
+    FULL: {
+        (1, 0): [(D0, 5), (U1, 3), (O, 3)],
+        (2, 1): [(D0, 6), (U0, 3), (D1, 7)],
+        (2, 4): [(U1, 5), (O, 4)],
     },
-    "close": {
-        (0,): ["u1.p2", "o.p2"],
-        (1,): ["dw0", "u1.p3", "d1.p4", "u0.p2"],
-        (2,): ["dw1", "gh1", "gh0", "o.p4", "d0.p6", "d1.p5", "ghA"],
+    DIAGONAL: {
+        (1, 0): [(D1, 6)],
+        (2, 1): [(D0, 7)],
     },
-    "diagonal": {
-        (2, 1): ["u1.p4"],
-        (2, 2): ["u0.p3"],
-        (2, 3): ["q0.p2"],
+    CLOSE: {
+        (1,): [(U1, 4), (SEND, 0)],
+        (2,): [(Q0, 3), (SEND, 1), (GRAD_H, 0), (U0, 4), (GRAD_H, 1), (GRAD_H, 2), (O, 5), (U1, 6)],
     },
-    "end": {
-        (): ["ghx", "ghB", "q1.p2", "ghC", "u1.p4b", "u0.p4", "q0.p3", "o.p4b", "u1.p5", "d1.p6", "q0.p4", "u0.p4b", "q1.p3", "o.p5", "final", "u1.p6", "q0.p4b", "u0.p5", "o.p6", "q1.p4", "q0.p5", "u0.p6", "q1.p4b", "q1.p5", "q0.p6", "q1.p6"],
+    END: {
+        (): [(GRAD_H, 3), (Q1, 3), (D1, 8), (GRAD_H, 4), (GRAD_H, 5), (Q0, 4), (U0, 5), (D0, 8),
+            (O, 6), (Q1, 4), (U1, 7), (Q0, 5), (O, 7), (U0, 6), (Q1, 5), (GRAD_H, 6),
+            (U1, 8), (O, 8), (Q0, 6), (U0, 7), (Q1, 6), (Q0, 7), (Q1, 7), (U0, 8),
+            (Q0, 8), (Q1, 8)],
     },
 }
 
 
-def back_sums(n, width, share, part, mine):
-    half = [("d%d" % k, ("half", "share")[k], n > 8 or FAR_Z["d"], k, 0, part, width) for k in range(2)]
-    up = [("u%d" % k, U_MODES[k], n > 8 or FAR_Z["u"], 0, k * part, part, width) for k in range(2)]
-    out = [("o", O_MODE, n > 8 or FAR_Z["o"], 1, 0, 2 * share, part)]
-    return half + up + out + [
-        ("q%d" % k, "share", n > 8 or FAR_Z["q"], None, 0, width // share * mine, mine * len(hs)) for k, hs in enumerate(Q_HEADS)
-    ]
+def folds(cols):
+    return 2 if cols % 128 else 1
+
+
+def back_sums(n, width, share, part):
+    way = lambda k: QUARTERS if n > 8 else WAYS[k]
+    half = [(D0 + k, ("half", "ready")[k], way(D0 + k), k, 0, part, width) for k in range(2)]
+    up = [(U0 + k, U_MODES[k], way(U0 + k), 0, k * part, part, width) for k in range(2)]
+    sums = half + up + [(O, O_MODE, way(O), 1, 0, 2 * share, part)]
+    for k, hs in enumerate(Q_HEADS):
+        cols = share * len(hs)
+        sums.append((Q0 + k, "share", way(Q0 + k), None, 0, width // folds(cols), cols * folds(cols)))
+    return sums
 
 
 def back_kernel(n, tok, blocks, heads, parts, *refs):
     refs = list(refs)
     take = lambda count: [refs.pop(0) for _ in range(count)]
     hbm = dict(zip(BACK_IN, take(len(BACK_IN))))
-    down_half, down_share, gu, go, w_qkv, w_up, gain_one, gain_two = take(8)
-    down_o, up_o, out_o, qkv_o, gain_one_o, gain_two_o, rg_o = take(7)
+    down_half, down_ready, gu, go, gain_one = take(5)
+    down_o, up_o, out_o, rg_o = take(4)
+    qkv_o = take(len(Q_HEADS))
     vm = dict(zip(BACK_IN, take(len(BACK_IN))))
-    dkT, dvT, delta, dP, prior_out, prior_in, g_stage, g_core, g_x, g_acc, qkv_v, wq_rows, wu_rows, gcol = take(14)
+    dkT, dvT, delta, dP, prior_out, prior_in, g_stage, g_core, g_x, g_acc = take(10)
     dws = take(len(Q_HEADS))
     p, hd, row = Place(n), HD, blocks * tok
     mine, width = heads * hd, blocks * heads * hd
     share, part = width // blocks, width // 2
     per_part = part // share
-    outs = {"d%d" % k: [(pl.ds(0, part), down_o.at[pl.ds(k * part, part)])] for k in range(2)}
+    outs = {D0 + k: [(pl.ds(0, part), down_o.at[pl.ds(k * part, part)])] for k in range(2)}
     for k in range(2):
-        outs["u%d" % k] = [
+        outs[U0 + k] = [
             (pl.ds(j * share, share), up_o.at[:, pl.ds((k * per_part + j) * width, width)]) for j in range(per_part)
         ]
-    outs["o"] = [(pl.ds(k * share, share), out_o.at[:, pl.ds(k * part, part)]) for k in range(2)]
-    plans = back_sums(n, width, share, part, mine)
-    bufs = [take(len(Sum.scratch(q[1], q[2], 16, 128, n, q[0] in outs))) for q in plans]
+    outs[O] = [(pl.ds(k * share, share), out_o.at[:, pl.ds(k * part, part)]) for k in range(2)]
+    for k in range(len(Q_HEADS)):
+        outs[Q0 + k] = [(pl.ds(0, qkv_o[k].shape[0]), qkv_o[k])]
+    plans = back_sums(n, width, share, part)
+    bufs = [take(len(Sum.scratch(q[1], q[2], 16, 128, n))) for q in plans]
     c = Copies(refs.pop(0))
     for name in BACK_IN:
         src = (lambda: hbm["x"].at[:, 0, :]) if name == "x" else (lambda name=name: hbm[name])
         c.local(name, src, lambda name=name: vm[name])
-    c.local("wq rows", lambda: w_qkv.at[rows_at(p.s * share, share)], lambda: wq_rows)
-    c.local("wu rows", lambda: w_up.at[rows_at(p.s * share, share)], lambda: wu_rows)
     sums = {}
-    for (name, mode, far_z, arr, first, rows, cols), buf in zip(plans, bufs):
-        src = None if arr is None else ((down_half, down_share) if name[0] == "d" else (gu, go))[arr]
-        sums[name] = Sum(p, c, name, mode, far_z, src, first, rows, cols, buf, outs.get(name, []))
-    qkv = [sums["q%d" % k] for k in range(len(Q_HEADS))]
-    for k, own in enumerate(qkv):
-        spot = lambda own=own: own.own.at[0, rows_at(p.s * mine, mine)]
+    for (name, mode, way, arr, first, rows, cols), buf in zip(plans, bufs):
+        src = None if arr is None else ((down_half, down_ready) if name < U0 else (gu, go))[arr]
+        sums[name] = Sum(p, c, name, mode, way, src, first, rows, cols, buf, outs[name])
+    qkv = [sums[Q0 + k] for k in range(len(Q_HEADS))]
+    for k, one in enumerate(qkv):
+        count = one.rows // blocks
+        block = lambda ref, s, count=count: ref.at[rows_at(s * count, count)]
+        spot = lambda one=one, block=block: block(one.own.at[0], p.s)
         for what, mate in (("cross", p.cross_mate), ("chip", p.chip_mate), ("core", p.core_mate)):
-            c.remote(("dw", k, what), lambda k=k, mate=mate: dws[k].at[rows_at(mate()[0] * mine, mine)], spot, mate)
-        c.local(("dw", k, "own"), lambda k=k: dws[k].at[rows_at(p.s * mine, mine)], spot)
+            c.remote(("dw", k, what), lambda k=k, mate=mate, block=block: block(dws[k], mate()[0]), spot, mate)
+        c.local(("dw", k, "own"), lambda k=k, block=block: block(dws[k], p.s), spot)
     for k in range(heads):
         c.remote(("prior", k), lambda k=k: prior_out.at[k], lambda k=k: prior_in.at[k], p.prior_row)
     for order in (1, 0):
         c.remote(("gh", order), lambda order=order: g_stage.at[order], lambda order=order: g_core.at[order], p.core_mate)
     c.remote(("gh", "x"), lambda: g_stage.at[1], lambda: g_x, p.chip_mate)
     c.local("rg", lambda: vm["gm"], lambda: rg_o.at[:, 0, :])
-    c.local("qkv", lambda: qkv_v, lambda: qkv_o)
 
     def grad_h_part(owner):
         return dot(vm["wm"][...], dP[:, pl.ds(pl.multiple_of(owner * tok, tok), tok)])
@@ -892,35 +927,43 @@
 
     def send_dw(k):
         rows = slice(Q_HEADS[k][0] * 3 * hd, (Q_HEADS[k][-1] + 1) * 3 * hd)
-        dws[k][...] = dot_nt(vm["hT"][...], dP[rows, :]).astype(BF16)
+        grad = dot_nt(vm["hT"][...], dP[rows, :]).astype(BF16)
+        fold = folds(grad.shape[1])
+        count = share // fold
+        for s in range(blocks):
+            cells = [grad[s * share + f * count : s * share + (f + 1) * count] for f in range(fold)]
+            dws[k][s * count : (s + 1) * count, :] = jnp.concatenate(cells, axis=1)
         c.start(*[("dw", k, what) for what in DW])
 
-    steps = {"gh1": lambda: core_grad(1), "gh0": lambda: core_grad(0), "ghA": lambda: keep_grad(1), "ghx": chip_grad}
-    steps.update({"ghB": lambda: keep_grad(0), "ghC": own_grad, "final": input_grad})
-    for name, one in sums.items():
-        for phase in ("p0", "p1", "p1b", "p2", "p3", "p4", "p4b", "p5", "p6"):
-            steps[name + "." + phase] = getattr(one, phase)
-    for k in range(len(Q_HEADS)):
-        steps["dw%d" % k] = lambda k=k: send_dw(k)
-        steps["q%d.p2" % k] = lambda k=k: (c.wait(*[("dw", k, what) for what in DW]), qkv[k].p2())
-
-    def steps_at(place, **now):
+    special = {GRAD_H: [lambda: core_grad(1), lambda: core_grad(0), lambda: keep_grad(1), chip_grad, lambda: keep_grad(0)]}
+    special[GRAD_H] += [own_grad, input_grad]
+    special[SEND] = [lambda k=k: send_dw(k) for k in range(len(Q_HEADS))]
+
+    def step(which, phase):
+        if which in special:
+            special[which][phase]()
+            return
+        if which >= Q0 and phase == 3:
+            c.wait(*[("dw", which - Q0, what) for what in DW])
+        sums[which].phase(phase)
+
+    def steps_at(place, *now):
         for at, names in PLAN.get(place, {}).items():
             same = None
-            for want, have in zip(at, now.values()):
+            for want, have in zip(at, now):
                 same = (have == want) if same is None else same & (have == want)
 
             def run():
-                for name in names:
-                    steps[name]()
+                for which, phase in names:
+                    step(which, phase)
 
             run() if same is None else pl.when(same)(run)
 
     first = BACK_IN[:8]
     c.start(*first)
     greet(p.all_mates())
-    steps_at("start")
-    c.start(*BACK_IN[8:], "wq rows", "wu rows")
+    steps_at(START)
+    c.start(*BACK_IN[8:])
     c.wait(*first)
     dqT = vm["oT"]
     doT, kk, vv, kT, qT, lse, start = (vm[x] for x in ("doT", "k", "v", "kT", "qT", "lse", "start"))
@@ -934,7 +977,7 @@
     dqT[...] = jnp.zeros_like(dqT)
     dkT[...] = jnp.zeros_like(dkT)
     dvT[...] = jnp.zeros_like(dvT)
-    steps_at("ready")
+    steps_at(READY)
 
     def pair(h, i, j, causal):
         hr = pl.ds(pl.multiple_of(h * hd, hd), hd)
@@ -962,7 +1005,7 @@
             @pl.when(h == k)
             def _():
                 c.start(("prior", k))
-        steps_at("prior", h=h)
+        steps_at(PRIOR, h)
         return carry
 
     lax.fori_loop(0, heads, prior, 0)
@@ -983,14 +1026,14 @@
             i = jnp.where(t < 3, 3, jnp.where(t < 5, 2, 1))
             j = jnp.where(t < 3, t + 1, jnp.where(t < 5, t - 2, 1))
             pair(h, i, j, False)
-            steps_at("full", h=h, t=t)
+            steps_at(FULL, h, t)
             return carry
 
         lax.fori_loop(0, 6, full, 0)
 
         def diagonal(i, carry):
             pair(h, i, i + 1, True)
-            steps_at("diagonal", h=h, i=i)
+            steps_at(DIAGONAL, h, i)
             return carry
 
         lax.fori_loop(0, blocks, diagonal, 0)
@@ -1001,80 +1044,130 @@
                     c.wait("hT", "wm")
                 c.wait(("prior", k))
         close(h)
-        steps_at("close", h=h)
+        steps_at(CLOSE, h)
         return carry
 
     lax.fori_loop(0, heads, head, 0)
-    steps_at("end")
-
-    def row_of(col):
-        return jnp.broadcast_to(col, (share, 128)).T[0:1, :]
-
-    def my_gain(gain):
-        gcol[...] = column(gain)
-        return gcol[pl.ds(pl.multiple_of(p.s * share, share), share), :]
-
-    c.wait("wq rows", "wu rows")
-    total = jnp.zeros((share, 1), F32)
-    for k in range(2):
-        for j in range(per_part):
-            cols = slice((k * per_part + j) * width, (k * per_part + j + 1) * width)
-            prod = sums["u%d" % k].full[j * share : (j + 1) * share, :] * wu_rows[:, cols].astype(F32)
-            total = total + jnp.sum(prod, axis=1, keepdims=True)
-    gain_two_o[...] = row_of(total / my_gain(gain_two))
-    total = jnp.zeros((share, 1), F32)
-    for k in range(3):
-        for s in range(blocks):
-            cells = []
-            for own, hs in zip(qkv, Q_HEADS):
-                for h in range(len(hs)):
-                    at = (h * 3 + k) * hd
-                    cells.append(own.res[s * share : (s + 1) * share, at : at + hd])
-            cells = jnp.concatenate(cells, axis=1).astype(F32)
-            cols = slice(k * width + s * mine, k * width + (s + 1) * mine)
-            qkv_v[:, cols] = cells
-            total = total + jnp.sum(cells * wq_rows[:, cols].astype(F32), axis=1, keepdims=True)
-    gain_one_o[...] = row_of(total / my_gain(gain_one))
-    c.start("qkv")
+    steps_at(END)
+
     for one in sums.values():
         one.p7()
-    c.wait("qkv", "rg")
-
-
-def back_pass(n, tok, blocks, ins, down_half, down_share, gu, go, w_qkv, w_up, gain_one, gain_two):
+    c.wait("rg")
+
+
+def back_pass(n, tok, blocks, ins, down_half, down_ready, gu, go, gain, parts):
     heads = ins[1].shape[0]
     row = blocks * tok
     width = ins[8].shape[0]
     mine = heads * HD
-    parts, share, part = w_up.shape[1] // width, width // blocks, width // 2
+    share, part = width // blocks, width // 2
     v = lambda *s, t=BF16: pltpu.VMEM(s, t)
-    o = lambda *s: jax.ShapeDtypeStruct(s, F32)
+    o = lambda *s, t=BF16: jax.ShapeDtypeStruct(s, t)
     scratch = [v(width - 1, tok, t=F32) if name == "x" else pltpu.VMEM(a.shape, a.dtype) for name, a in zip(BACK_IN, ins)]
     scratch += [
         v(mine, row + tok, t=F32), v(mine, row + tok, t=F32), v(heads, 1, row, t=F32), v(3 * mine, row),
         v(heads, 2 * HD, tok), v(heads, 2 * HD, tok),
-        v(2, width, tok), v(2, width, tok), v(width, tok), v(width, tok, t=F32), v(share, 3 * width, t=F32),
-        v(share, 3 * width), v(share, w_up.shape[1]), v(width, 1, t=F32),
+        v(2, width, tok), v(2, width, tok), v(width, tok), v(width, tok, t=F32),
     ]
-    scratch += [v(width, mine * len(hs)) for hs in Q_HEADS]
+    sums = back_sums(n, width, share, part)
+    scratch += [v(*one[5:]) for one in sums[Q0:]]
     copies = len(ins) + 5 * heads + 8
-    for name, mode, far_z, _, _, rows, cols in back_sums(n, width, share, part, mine):
-        scratch += Sum.scratch(mode, far_z, rows, cols, n, name[0] != "q")
+    for _, mode, way, _, _, rows, cols in sums:
+        scratch += Sum.scratch(mode, way, rows, cols, n)
         copies += 17 + n // 8
     scratch.append(pltpu.SemaphoreType.DMA((2, copies)))
     hbm = pl.BlockSpec(memory_space=pl.ANY)
     vmem = pl.BlockSpec(memory_space=pltpu.VMEM)
     return pl.pallas_call(
         functools.partial(back_kernel, n, tok, blocks, heads, parts),
-        out_shape=[
-            o(width, width), o(share, parts * width), o(share, width), o(share, 3 * width),
-            o(1, share), o(1, share), o(width - 1, 1, tok),
-        ],
-        in_specs=[hbm] * (len(ins) + 6) + [vmem, vmem],
-        out_specs=[hbm] * 4 + [vmem, vmem, hbm],
+        out_shape=[o(width, width), o(share, parts * width), o(share, width), o(width - 1, 1, tok, t=F32)]
+        + [o(*one[5:]) for one in sums[Q0:]],
+        in_specs=[hbm] * (len(ins) + 4) + [vmem],
+        out_specs=[hbm] * (4 + len(Q_HEADS)),
         scratch_shapes=scratch,
         compiler_params=pltpu.CompilerParams(collective_id=1, has_side_effects=True, vmem_limit_bytes=VMEM_LIMIT),
-    )(*ins, down_half, down_share, gu, go, w_qkv, w_up, gain_one, gain_two)
+    )(*ins, down_half, down_ready, gu, go, gain)
+
+
+def last_kernel(blocks, *refs):
+    new, rg, down, up, out, w_qkv, w_up, gain_one, gain_two = refs[:9]
+    q_in = refs[9 : 9 + len(Q_HEADS)]
+    refs = refs[9 + len(Q_HEADS) :]
+    new_o, rg_o, gain_one_o, gain_two_o, qkv_o, out_o, up_o, down_o = refs[:8]
+    down_v, up_v, out_v, wq, wu, gcol, down_f, up_f, out_f, qkv_f, x_v, sems = refs[8:19] + refs[-1:]
+    q_v = refs[19:-1]
+    s = lax.axis_index("seq")
+    share, width = out_v.shape
+    mine, hd = width // blocks, HD
+    c = Copies(sems)
+    my_rows = lambda ref: ref.at[rows_at(s * share, share)]
+    loads = list(zip(q_in, q_v)) + [(my_rows(w_qkv), wq), (up, up_v), (down, down_v), (out, out_v), (my_rows(w_up), wu)]
+    for k, (src, dst) in enumerate(loads):
+        c.local(("in", k), lambda src=src: src, lambda dst=dst: dst)
+    for k, (src, dst) in enumerate(((up_f, up_o), (down_f, down_o), (out_f, out_o), (qkv_f, qkv_o))):
+        c.local(("out", k), lambda src=src: src, lambda dst=dst: dst)
+    for k, (src, dst) in enumerate(((new, new_o), (rg, rg_o))):
+        c.local(("x in", k), lambda k=k, src=src: src.at[:, 0, :], lambda k=k: x_v.at[k])
+        c.local(("x out", k), lambda k=k: x_v.at[k], lambda k=k, dst=dst: dst.at[:, 0, :])
+    at = len(q_in)
+    c.start(*[("in", k) for k in range(at + 2)], ("x in", 0), ("x in", 1), *[("in", k) for k in range(at + 2, len(loads))])
+
+    def row_of(col):
+        return jnp.broadcast_to(col, (share, 128)).T[0:1, :]
+
+    def my_gain(gain):
+        gcol[...] = column(gain)
+        return gcol[pl.ds(pl.multiple_of(s * share, share), share), :]
+
+    c.wait(*[("in", k) for k in range(at + 1)])
+    total = jnp.zeros((share, 1), F32)
+    for k in range(3):
+        for o in range(blocks):
+            cells = []
+            for src, hs in zip(q_v, Q_HEADS):
+                fold, cols = folds(share * len(hs)), share * len(hs)
+                rows = slice(o * share // fold, (o + 1) * share // fold)
+                for h in range(len(hs)):
+                    lanes = [f * cols + (h * 3 + k) * hd for f in range(fold)]
+                    cells.append(jnp.concatenate([src[rows, lane : lane + hd] for lane in lanes], axis=0))
+            cells = jnp.concatenate(cells, axis=1).astype(F32)
+            cols = slice(k * width + o * mine, k * width + (o + 1) * mine)
+            qkv_f[:, cols] = cells
+            total = total + jnp.sum(cells * wq[:, cols].astype(F32), axis=1, keepdims=True)
+    c.start(("out", 3))
+    for k, (src, dst) in enumerate(((up_v, up_f), (down_v, down_f), (out_v, out_f))):
+        c.wait(("in", at + 1 + k))
+        dst[...] = src[...].astype(F32)
+        c.start(("out", k))
+        if k < 2:
+            c.wait(("x in", k))
+            c.start(("x out", k))
+    c.wait(("in", at + 4))
+    gain_two_o[...] = row_of(jnp.sum(up_f[...] * wu[...].astype(F32), axis=1, keepdims=True) / my_gain(gain_two))
+    gain_one_o[...] = row_of(total / my_gain(gain_one))
+    c.wait(("x out", 0), ("x out", 1), *[("out", k) for k in range(4)])
+
+
+def last_pass(blocks, new, rg, down, up, out, qs, w_qkv, w_up, gain_one, gain_two):
+    share, width = out.shape
+    v = lambda *s, t=BF16: pltpu.VMEM(s, t)
+    f = lambda *s: jax.ShapeDtypeStruct(s, F32)
+    hbm = pl.BlockSpec(memory_space=pl.ANY)
+    vmem = pl.BlockSpec(memory_space=pltpu.VMEM)
+    scratch = [
+        v(*down.shape), v(*up.shape), v(*out.shape), v(share, 3 * width), v(*up.shape), v(width, 1, t=F32),
+        v(*down.shape, t=F32), v(*up.shape, t=F32), v(*out.shape, t=F32), v(share, 3 * width, t=F32),
+        v(2, new.shape[0], new.shape[2], t=F32),
+    ]
+    scratch += [v(*q.shape) for q in qs] + [pltpu.SemaphoreType.DMA((1, 20))]
+    return pl.pallas_call(
+        functools.partial(last_kernel, blocks),
+        out_shape=[f(*new.shape), f(*rg.shape), f(1, share), f(1, share), f(share, 3 * width), f(*out.shape), f(*up.shape), f(*down.shape)],
+        in_specs=[hbm] * 7 + [vmem] * 2 + [hbm] * len(qs),
+        out_specs=[hbm, hbm, vmem, vmem] + [hbm] * 4,
+        scratch_shapes=scratch,
+        compiler_params=pltpu.CompilerParams(vmem_limit_bytes=VMEM_LIMIT),
+    )(new, rg, down, up, out, w_qkv, w_up, gain_one, gain_two, *qs)
 
 
 def per_device(residual, documents, gain_one, gain_two, w_qkv, w_out, w_up, w_down, cotangent):
@@ -1084,12 +1177,15 @@
     x = jnp.transpose(residual, (2, 0, 1))
     cot = jnp.transpose(cotangent, (2, 0, 1))
     attT, hT, kT, qT, oT, lse, start, k, v, w_mine = fore_pass(n, tok, blocks, x, gain_one, documents, w_qkv)
-    new, grad_middle, doT, grad_up, grad_out, down_half, down_share = mid_pass(
+    new, grad_middle, doT, grad_up, grad_out, down_half, down_ready = mid_pass(
         n, blocks, x, cot, attT, gain_two, w_out, w_up, w_down
     )
-    sum_down, sum_up, sum_out, sum_qkv, one, two, grad_x = back_pass(
+    sum_down, sum_up, sum_out, grad_x, *sum_qkv = back_pass(
         n, tok, blocks, (doT, k, v, kT, qT, oT, lse, start, hT, w_mine, x, grad_middle),
-        down_half, down_share, grad_up, grad_out, w_qkv, w_up, gain_one, gain_two,
+        down_half, down_ready, grad_up, grad_out, gain_one, w_up.shape[1] // w_up.shape[0],
+    )
+    new, grad_x, one, two, sum_qkv, sum_out, sum_up, sum_down = last_pass(
+        blocks, new, grad_x, sum_down, sum_up, sum_out, sum_qkv, w_qkv, w_up, gain_one, gain_two
     )
     new, grad_x = jnp.transpose(new, (1, 2, 0)), jnp.transpose(grad_x, (1, 2, 0))
     return (new, grad_x, one[0], two[0], sum_qkv, sum_out, sum_up, sum_down)

time: 200 us -> 184 us (0.920)
  local copies, waits for them, and re-layouts: 10.8 us -> 0 us
  Pallas kernels: 188 us -> 182 us
    pallas_call x1, Pallas kernels: 105 us -> 90.3 us  [back_pass(): pl.pallas_call(functools.partial(back_kernel, n, tok, blocks, heads, part...]
    unnamed x24 -> x0, local copies, waits for them, and re-layouts: 10.8 us -> none
    pallas_call x0 -> x1, Pallas kernels: none -> 8.67 us  [last_pass(): pl.pallas_call(functools.partial(last_kernel, blocks), out_shape=[f(*new....]
where the time goes in v2:
time: 184 us; the launch traced here: 183 us
  Pallas kernels  182 us (99%)
    pallas_call x1, Pallas kernels, back_pass(): pl.pallas_call(functools.partial(back_kernel, n, tok, blocks, heads, part...  90.3 us
    pallas_call x1, Pallas kernels, fore_pass(): pl.pallas_call(functools.partial(fore_kernel, n, tok, blocks, heads), out...  45.2 us
    pallas_call x1, Pallas kernels, mid_pass(): pl.pallas_call(functools.partial(mid_kernel, n, blocks), out_shape=[o(wid...  37.9 us
    pallas_call x1, Pallas kernels, last_pass(): pl.pallas_call(functools.partial(last_kernel, blocks), out_shape=[f(*new....  8.67 us

profile of v2, /device:TPU:0, one launch (start us, length us, event | category | flops | bytes accessed | tf_op | source)
XLA Modules:
  0.0 183.0 jit_solution(212831837778170823)
XLA Ops:
  0.6 45.2 %shard_map.152 = (bf16[768,512]{1,0:T(8,128)(2,1)}, bf16[768,2048]{1,0:T(8,128)(2,1)}, bf16[192,2560]{1,0:T(8,128)(2,1)}, bf16[192,2048]{1,0:T(8,128)(2,1)}, f32...) custom-call(f32[767,1,512]{2,1,0:T(1,128)} %bitcast.6, ...), custom_call_target="tpu_custom_call" | custom-call | tf_op jit(solution)/shard_map/pallas_call | solution.py:612
  45.9 37.9 %shard_map.153 = (f32[767,1,512]{2,1,0:T(1,128)}, f32[767,512]{1,0:T(8,128)}, bf16[192,2048]{1,0:T(8,128)(2,1)}, bf16[4,768,768]{2,1,0:T(8,128)(2,1)}, bf16[4,38...) custom-call(f32[767,1,512]{2,1,0:T(1,128)} %bitcast.7, f32[767,1,512]{2,1,0:T(1,128)} %bitcast.9, ...), custom_call_target="tpu_custom_call" | custom-call | tf_op jit(solution)/shard_map/pallas_call | solution.py:785
  83.8 90.3 %shard_map.154 = (bf16[768,768]{1,0:T(8,128)(2,1)}, bf16[192,3072]{1,0:T(8,128)(2,1)}, bf16[192,768]{1,0:T(8,128)(2,1)}, f32[767,1,512]{2,1,0:T(1,128)}, bf16[76...) custom-call(bf16[192,2048]{1,0:T(8,128)(2,1)} %get-tuple-element.41.refs_0_, bf16[3,2560,64]{2,1,0:T(8,128)(2,1)} %get-tuple-element.42.refs_1_, ...), custom_call_target="tpu_custom_call" | custom-call | tf_op jit(solution)/shard_map/pallas_call | solution.py:1081
  174.1 8.7 %shard_map.155 = (f32[767,1,512]{2,1,0:T(1,128)}, f32[767,1,512]{2,1,0:T(1,128)}, f32[1,192]{1,0:T(1,128)}, f32[1,192]{1,0:T(1,128)}, f32[192,2304]{1,0:T(8,128)...) custom-call(f32[767,1,512]{2,1,0:T(1,128)} %get-tuple-element.40.refs_0_, ...), custom_call_target="tpu_custom_call" | custom-call | tf_op jit(solution)/shard_map/pallas_call | solution.py:1163
